TPU v7x, 768 devices: a whole 4x8x12 slice. The times are simulated.
768 devices in a mesh: blk: 32 (over z_lo, x, core), cap: 24 (over z_hi, y).
Axes of the slice: x: 4, y: 8, z: 12 (z_hi: 3, z_lo: 4; z = z_hi * 4 + z_lo), core: 2. Of those that a mesh axis runs over, the one named last changes fastest.
Arguments:
- image_emb: bfloat16 [36864, 1152], P(('blk', 'cap')), may hold values from -0.4375 to 0.4375
- text_emb: bfloat16 [36864, 1152], P(('blk', 'cap')), may hold values from -0.4375 to 0.4375
- caption_emb: bfloat16 [294912, 1152], P(('blk', 'cap')), may hold values from -0.4375 to 0.4375
- logit_scale: float32 [1], replicated, may hold values from 8 to 32
- logit_bias: float32 [1], replicated, may hold values from -4 to -2
- caption_owner: int32 [294912], P(('blk', 'cap')), may hold values from 0 to 47, as said below
- caption_valid: int32 [294912], P(('blk', 'cap')), may hold values from 0 to 1, as said below
- caption_count: int32 [36864], P(('blk', 'cap')), may hold values from 0 to 8, as said below
Outputs:
- row_loss: float32 [36864], P(('blk', 'cap'))
- image_grad: float32 [36864, 1152], P(('blk', 'cap'))
- text_grad: float32 [36864, 1152], P(('blk', 'cap'))
- caption_grad: bfloat16 [294912, 1152], P(('blk', 'cap'))
Inputs may be any that keep to these rules, and one draw needn't show every extreme that they name: `caption_owner`: each image owns exactly 8 of the 384 slots arriving at its device; every local row is an owner. `caption_valid`: an image's valid slots number exactly its caption_count. `caption_count`: every device holds an image with 8 extra captions.
All inputs are finite; a program needn't handle non-finite values.
Results may differ from a plain program's by a relative error of at most 0.011.
Values may be sent and summed in bfloat16 or wider, within the bound.
No kernel may reach another device: no remote copies, remote signals or barrier semaphores. Data moves between devices by JAX's collectives and lax.ppermute only.
A program may use at most 32 MiB of HBM per device.

v0:
```python
import jax
import jax.numpy as jnp
from jax import lax
from jax.sharding import PartitionSpec as P


def pair_coeff(left, right, left_first, scale, bias):
    logits = scale * jnp.dot(left, right.T, preferred_element_type=jnp.float32) + bias
    left_index = left_first + lax.broadcasted_iota(jnp.int32, logits.shape, 0)
    right_index = lax.broadcasted_iota(jnp.int32, logits.shape, 1)
    signs = jnp.where(left_index == right_index, jnp.float32(1.0), jnp.float32(-1.0))
    losses = jnp.sum(jax.nn.softplus(-signs * logits), axis=1)
    coeff = (-signs * jax.nn.sigmoid(-signs * logits)).astype(jnp.bfloat16)
    return (losses, coeff)


def shards(
    image_emb,
    text_emb,
    caption_emb,
    logit_scale,
    logit_bias,
    caption_owner,
    caption_valid,
    caption_count,
):
    scale = logit_scale[0]
    bias = logit_bias[0]
    rows = image_emb.shape[0]
    width = image_emb.shape[1]
    groups = lax.axis_size("cap")
    own_first = lax.axis_index("blk") * rows
    piece = lax.all_gather(text_emb, "blk", axis=0, tiled=True)
    row_loss, coeff = pair_coeff(image_emb, piece, own_first, scale, bias)
    part = jnp.dot(coeff, piece, preferred_element_type=jnp.float32)
    loss_sum = row_loss
    text_grad = scale * lax.psum_scatter(
        jnp.dot(coeff.T, image_emb, preferred_element_type=jnp.float32),
        "blk",
        scatter_dimension=0,
        tiled=True,
    )
    slot_rows = caption_emb.shape[0] // groups
    outgoing = caption_emb.reshape(groups, slot_rows, width)
    arrived = lax.all_to_all(outgoing, "cap", split_axis=0, concat_axis=0, tiled=True).reshape(
        groups * slot_rows, width
    )
    select = caption_owner[:, None] == jnp.arange(rows, dtype=jnp.int32)[None, :]
    select_f = select.astype(jnp.float32)
    picked = jnp.dot(select.astype(jnp.bfloat16), image_emb, preferred_element_type=jnp.float32)
    cap_logit = scale * jnp.sum(picked * arrived.astype(jnp.float32), axis=1) + bias
    owner_count = jnp.dot(select_f, caption_count.astype(jnp.float32))
    denom = jnp.maximum(owner_count, 1.0)
    flags = caption_valid.astype(jnp.float32)
    cap_loss = flags * jax.nn.softplus(-cap_logit) / denom
    cap_coeff = (flags * (jax.nn.sigmoid(cap_logit) - 1.0) / denom).astype(jnp.bfloat16)
    extra = jnp.dot(cap_loss, select_f)
    weights = (select_f * cap_coeff.astype(jnp.float32)[:, None]).astype(jnp.bfloat16)
    cap_part = jnp.dot(weights.T, arrived, preferred_element_type=jnp.float32)
    cap_grad = (scale * cap_coeff.astype(jnp.float32)[:, None] * picked).astype(jnp.bfloat16)
    returned = lax.all_to_all(
        cap_grad.reshape(groups, slot_rows, width), "cap", split_axis=0, concat_axis=0, tiled=True
    )
    row_loss = loss_sum + extra
    image_grad = scale * (part + cap_part)
    return (row_loss, image_grad, text_grad, returned.reshape(groups * slot_rows, width))


def solution(mesh):
    in_specs = (
        P(("blk", "cap"), None),
        P(("blk", "cap"), None),
        P(("blk", "cap"), None),
        P(),
        P(),
        P(("blk", "cap")),
        P(("blk", "cap")),
        P(("blk", "cap")),
    )
    out_specs = (
        P(("blk", "cap")),
        P(("blk", "cap"), None),
        P(("blk", "cap"), None),
        P(("blk", "cap"), None),
    )
    return jax.shard_map(shards, mesh=mesh, in_specs=in_specs, out_specs=out_specs, check_vma=False)
```

profile of v0, /device:TPU:1, one launch (start us, length us, event | category | flops | bytes accessed | tf_op | source)
XLA Modules:
  0.0 286.4 jit_solution(16076295770314007392)
XLA Ops:
  7.2 0.0 copy-start
  7.2 0.0 all-gather.2.cloned.1.call-start
  7.2 0.7 all-gather.2.cloned.1.call-update
  7.9 0.0 reduce-scatter.2.cloned.1.call-start
  9.3 77.0 %all-gather.2.cloned.1.call-done = bf16[1536,1152]{1,0:T(8,128)(2,1)} async-done(((bf16[48,1152]{1,0:T(8,128)(2,1)}), bf16[1536,1152]{1,0:T(8,128)(2,1)}) %all-gather.2.cloned.1.call-update) | async-done | bytes 3538960 | tf_op jit(solution)/shard_map/all_gather | solution.py:33
  86.3 0.0 copy-done
  86.3 3.3 %fusion.4 = (f32[48]{0:T(128)S(1)}, f32[48,1536]{1,0:T(8,128)S(1)}) fusion(f32[]{:T(128)} %bitcast.26, bf16[48,1152]{1,0:T(8,128)(2,1)S(1)} %copy-done, bf16[1536,1152]{1,0:T(8,128)(2,1)} %all-gather.2.cloned.1.call-done, f32[]{:T(128)} %bitcast.21, s32[48]{0:T(128)S(1)} %iota_add_fusion), kind=kOutput, calls=%fused_computation.11 | convolution fusion | flops 170827728 | bytes 3944840 | tf_op jit(solution)/shard_map/dot_general | solution.py:8
  89.6 4.1 %fusion.20 = f32[1536,1152]{1,0:T(8,128)} fusion(bf16[48,1152]{1,0:T(8,128)(2,1)S(1)} %copy-done, f32[48,1536]{1,0:T(8,128)S(1)} %get-tuple-element.7, s32[48]{0:T(128)S(1)} %iota_add_fusion), kind=kOutput, calls=%fused_computation.38 | convolution fusion | flops 170459136 | bytes 7483584 | tf_op jit(solution)/shard_map/dot_general | solution.py:38
  93.8 0.0 reduce-scatter.2.cloned.1.call-update
  93.8 0.0 copy-start.1
  93.8 12.1 %all-to-all-start = ((bf16[24,16,1152]{2,1,0:T(8,128)(2,1)}), bf16[24,16,1152]{2,1,0:T(8,128)(2,1)S(1)}, u32[]{:S(2)}, u32[]{:S(2)}) async-start(bf16[24,16,1152]{2,1,0:T(8,128)(2,1)} %bitcast.2), calls=%async_computation | async-start | bytes 1769472 | tf_op jit(solution)/shard_map/all_to_all | solution.py:45
  105.9 0.0 copy-done.2
  105.9 0.2 convolution_reduce_fusion
  106.2 27.3 %all-to-all-done = bf16[24,16,1152]{2,1,0:T(8,128)(2,1)S(1)} async-done(((bf16[24,16,1152]{2,1,0:T(8,128)(2,1)}), bf16[24,16,1152]{2,1,0:T(8,128)(2,1)S(1)}, u32[]{:S(2)}, u32[]{:S(2)}) %all-to-all-start) | async-done | bytes 884768 | tf_op jit(solution)/shard_map/all_to_all | solution.py:45
  133.5 0.5 multiply_reduce_fusion
  134.1 1.1 multiply_convert_fusion
  135.2 5.7 %all-to-all-start.1 = ((bf16[24,16,1152]{2,1,0:T(8,128)(2,1)}), bf16[24,16,1152]{2,1,0:T(8,128)(2,1)S(1)}, u32[]{:S(2)}, u32[]{:S(2)}) async-start(bf16[24,16,1152]{2,1,0:T(8,128)(2,1)} %bitcast.6), calls=%async_computation.2 | async-start | bytes 1769472 | tf_op jit(solution)/shard_map/all_to_all | solution.py:61
  141.0 0.5 fusion.6
  141.4 19.2 %all-to-all-done.1 = bf16[24,16,1152]{2,1,0:T(8,128)(2,1)S(1)} async-done(((bf16[24,16,1152]{2,1,0:T(8,128)(2,1)}), bf16[24,16,1152]{2,1,0:T(8,128)(2,1)S(1)}, u32[]{:S(2)}, u32[]{:S(2)}) %all-to-all-start.1) | async-done | bytes 884768 | tf_op jit(solution)/shard_map/all_to_all | solution.py:61
  160.7 0.7 fusion.3
  161.4 3.5 %fusion = f32[48,1152]{1,0:T(8,128)} fusion(f32[48,1152]{1,0:T(8,128)S(1)} %fusion.6, bf16[1536,1152]{1,0:T(8,128)(2,1)} %all-gather.2.cloned.1.call-done, f32[]{:T(128)} %bitcast.23, f32[48,1536]{1,0:T(8,128)S(1)} %get-tuple-element.7, s32[48]{0:T(128)S(1)} %iota_add_fusion), kind=kOutput, calls=%fused_computation.1 | convolution fusion | flops 170569728 | bytes 4276420 | tf_op jit(solution)/shard_map/dot_general | solution.py:35
  164.9 112.1 %reduce-scatter.2.cloned.1.call-done = f32[48,1152]{1,0:T(8,128)} async-done(((f32[1536,1152]{1,0:T(8,128)}), f32[48,1152]{1,0:T(8,128)}) %reduce-scatter.2.cloned.1.call-update) | async-done | bytes 221200 | tf_op jit(solution)/shard_map/reduce_scatter | solution.py:37
  277.0 1.6 broadcast_multiply_fusion
  278.7 0.9 copy.15
  (8 shorter events, 0.1 us)
Async XLA Ops:
  7.2 79.1 %copy-start = (bf16[48,1152]{1,0:T(8,128)(2,1)S(1)}, bf16[48,1152]{1,0:T(8,128)(2,1)}, u32[]{:S(2)}) copy-start(bf16[48,1152]{1,0:T(8,128)(2,1)} %param.8) | copy-start | bytes 331780
  7.2 79.1 %all-gather.2.cloned.1.call-start = ((), (), s32[]{:S(2)}) async-start(), calls=%async_computation.3 | async-start | bytes 3649536 | tf_op jit(solution)/shard_map/all_gather | solution.py:33
  7.9 269.1 %reduce-scatter.2.cloned.1.call-start = ((), (), s32[]{:S(2)}) async-start(), calls=%async_computation.4 | async-start | bytes 7299072 | tf_op jit(solution)/shard_map/reduce_scatter | solution.py:37
  93.8 12.2 %copy-start.2 = (s32[384]{0:T(512)S(1)}, s32[384]{0:T(512)}, u32[]{:S(2)}) copy-start(s32[384]{0:T(512)} %param.13) | copy-start | bytes 4612
  93.8 12.2 %copy-start.3 = (s32[48]{0:T(128)S(1)}, s32[48]{0:T(128)}, u32[]{:S(2)}) copy-start(s32[48]{0:T(128)} %param.15) | copy-start | bytes 580
  93.8 40.3 %copy-start.1 = (s32[384]{0:T(512)S(1)}, s32[384]{0:T(512)}, u32[]{:S(2)}) copy-start(s32[384]{0:T(512)} %param.14) | copy-start | bytes 4612
  93.8 39.7 %all-to-all-start = ((bf16[24,16,1152]{2,1,0:T(8,128)(2,1)}), bf16[24,16,1152]{2,1,0:T(8,128)(2,1)S(1)}, u32[]{:S(2)}, u32[]{:S(2)}) async-start(bf16[24,16,1152]{2,1,0:T(8,128)(2,1)} %bitcast.2), calls=%async_computation | async-start | bytes 1769472 | tf_op jit(solution)/shard_map/all_to_all | solution.py:45
  135.2 25.5 %all-to-all-start.1 = ((bf16[24,16,1152]{2,1,0:T(8,128)(2,1)}), bf16[24,16,1152]{2,1,0:T(8,128)(2,1)S(1)}, u32[]{:S(2)}, u32[]{:S(2)}) async-start(bf16[24,16,1152]{2,1,0:T(8,128)(2,1)} %bitcast.6), calls=%async_computation.2 | async-start | bytes 1769472 | tf_op jit(solution)/shard_map/all_to_all | solution.py:61
Sparse Core Ops, SparseCore 0:
  10.5 75.7 all-gather.1
  93.9 183.0 reduce-scatter.1
where the time goes:
time: 289 us; the launch traced here: 286 us
  waiting for transfers between devices  236 us (82%)
  starting transfers between devices  17.9 us (6%)
  between operations  15.4 us (5%)
  matrix products  12.9 us (4%)
    reduce_scatter x1, waiting for transfers between devices, shards(): lax.psum_scatter(jnp.dot(coeff.T, image_emb, preferred_element_type=jnp.f...  112 us
    all_gather x1, waiting for transfers between devices, shards(): piece = lax.all_gather(text_emb, 'blk', axis=0, tiled=True)  77 us
    all_to_all x1, waiting for transfers between devices, shards(): lax.all_to_all(outgoing, 'cap', split_axis=0, concat_axis=0, tiled=True)  27.3 us
    all_to_all x1, waiting for transfers between devices, shards(): lax.all_to_all(cap_grad.reshape(groups, slot_rows, width), 'cap', split_a...  19.2 us
    all_to_all x1, starting transfers between devices, shards(): lax.all_to_all(outgoing, 'cap', split_axis=0, concat_axis=0, tiled=True)  12.1 us
  transfers between devices with their start and end apart: 4, of which 4 were waited for; matrix products, arithmetic and copies ran while one was open for 2% of the time, Pallas kernels for 0%

commit v1 on v0

v1 whole, which is shorter than its diff:
```python
import jax
import jax.numpy as jnp
from jax import lax
from jax.sharding import PartitionSpec as P

N_ZL, N_X, N_C = 4, 4, 2
N_ZH, N_Y = 3, 8
LANES = 128


def blk_of(zl, x, c):
    return (zl * N_X + x) * N_C + c


def shift_zl(k):
    return [
        (blk_of(z, x, c), blk_of((z + k) % N_ZL, x, c))
        for z in range(N_ZL) for x in range(N_X) for c in range(N_C)
    ]


def shift_x(k):
    return [
        (blk_of(z, x, c), blk_of(z, (x + k) % N_X, c))
        for z in range(N_ZL) for x in range(N_X) for c in range(N_C)
    ]


def swap_c():
    return [
        (blk_of(z, x, c), blk_of(z, x, 1 - c))
        for z in range(N_ZL) for x in range(N_X) for c in range(N_C)
    ]


def shift_zh(k):
    return [(h * N_Y + y, ((h + k) % N_ZH) * N_Y + y) for h in range(N_ZH) for y in range(N_Y)]


Y_GROUPS = [[h * N_Y + y for y in range(N_Y)] for h in range(N_ZH)]


def shards(image, text, caption, logit_scale, logit_bias, owner, valid, count):
    f32, bf16 = jnp.float32, jnp.bfloat16
    scale = logit_scale[0]
    bias = logit_bias[0]
    rows, width = image.shape
    slots = caption.shape[0]
    run = slots // (N_ZH * N_Y)
    third = slots // N_ZH
    zh = lax.axis_index("cap") // N_Y

    runs = caption.reshape(N_ZH, N_Y, run, width)
    order = [lax.rem(zh + (N_ZH - k), N_ZH) for k in range(N_ZH)]
    outgoing = jnp.stack([lax.dynamic_index_in_dim(runs, o, 0, False) for o in order], axis=1)
    arrived = lax.all_to_all(
        outgoing.reshape(N_Y, N_ZH * run, width), "cap", 0, 0, axis_index_groups=Y_GROUPS, tiled=True
    )
    arrived = arrived.reshape(N_Y, N_ZH, run, width)

    number = jnp.maximum(count, 1)
    holds = owner[None, :] == jnp.arange(rows, dtype=jnp.int32)[:, None]
    marks = jnp.where(holds & (valid[None, :] > 0), number[:, None], 0).astype(bf16)

    def with_marks(k):
        to = lax.rem(zh + k, N_ZH)
        part = lax.dynamic_slice_in_dim(marks, to * third, third, 1)
        return jnp.concatenate([image, part], axis=1)

    tagged = [with_marks(k) for k in range(N_ZH)]
    tagged = [tagged[0]] + [lax.ppermute(tagged[k], "cap", shift_zh(k)) for k in range(1, N_ZH)]

    texts = [text] + [lax.ppermute(text, "blk", shift_zl(k)) for k in range(1, N_ZL)]
    texts = jnp.concatenate(texts, axis=0)
    images = [image] + [lax.ppermute(image, "blk", shift_x(k)) for k in range(1, N_X)]
    images = jnp.concatenate(images, axis=0)
    images = jnp.concatenate([images, lax.ppermute(images, "blk", swap_c())], axis=0)

    logits = scale * jnp.dot(images, texts.T, preferred_element_type=f32) + bias
    left = lax.broadcasted_iota(jnp.int32, logits.shape, 0)
    right = lax.broadcasted_iota(jnp.int32, logits.shape, 1)
    signs = jnp.where((left == right) & (left < rows), f32(1.0), f32(-1.0))
    losses = jnp.sum(jax.nn.softplus(-signs * logits), axis=1)
    coeff = (-signs * jax.nn.sigmoid(-signs * logits)).astype(bf16)
    image_part = jnp.dot(coeff, texts, preferred_element_type=f32)
    text_part = jnp.dot(coeff.T, images, preferred_element_type=f32)

    def tag(grad, loss):
        high = loss.astype(bf16)
        low = (loss - high.astype(f32)).astype(bf16)
        lane = lax.broadcasted_iota(jnp.int32, (loss.shape[0], LANES), 1)
        extra = jnp.where(lane == 0, high[:, None], jnp.where(lane == 1, low[:, None], 0).astype(bf16))
        return jnp.concatenate([grad.astype(bf16), extra], axis=1)

    half = rows * N_X
    sent = tag(image_part, losses)
    got = lax.ppermute(sent[half:], "blk", swap_c()).astype(f32)
    grad_x = image_part[:half] + got[:, :width]
    loss_x = losses[:half] + got[:, width] + got[:, width + 1]
    sent = tag(grad_x, loss_x)
    image_sum = grad_x[:rows]
    loss_sum = loss_x[:rows]
    for k in range(1, N_X):
        back = lax.ppermute(sent[k * rows:(k + 1) * rows], "blk", shift_x(-k)).astype(f32)
        image_sum += back[:, :width]
        loss_sum += back[:, width] + back[:, width + 1]
    text_sum = text_part[:rows]
    for k in range(1, N_ZL):
        part = text_part[k * rows:(k + 1) * rows].astype(bf16)
        text_sum += lax.ppermute(part, "blk", shift_zl(-k)).astype(f32)

    cap_grads = []
    for k in range(N_ZH):
        e = arrived[:, k].reshape(third, width)
        i = tagged[k][:, :width]
        mark = tagged[k][:, width:].astype(f32)
        logit = scale * jnp.dot(i, e.T, preferred_element_type=f32) + bias
        there = mark > 0
        denom = jnp.where(there, mark, f32(1.0))
        loss = jnp.sum(jnp.where(there, jax.nn.softplus(-logit) / denom, 0.0), axis=1)
        weight = jnp.where(there, (jax.nn.sigmoid(logit) - 1.0) / denom, 0.0).astype(bf16)
        part = jnp.dot(weight, e, preferred_element_type=f32)
        cap_grads.append((scale * jnp.dot(weight.T, i, preferred_element_type=f32)).astype(bf16))
        if k == 0:
            image_sum += part
            loss_sum += loss
        else:
            back = lax.ppermute(tag(part, loss), "cap", shift_zh(-k)).astype(f32)
            image_sum += back[:, :width]
            loss_sum += back[:, width] + back[:, width + 1]
    back = jnp.stack([g.reshape(N_Y, run, width) for g in cap_grads], axis=1)
    back = lax.all_to_all(
        back.reshape(N_Y, N_ZH * run, width), "cap", 0, 0, axis_index_groups=Y_GROUPS, tiled=True
    )
    back = back.reshape(N_Y, N_ZH, run, width)
    place = [lax.rem(zh + (N_ZH - h), N_ZH) for h in range(N_ZH)]
    caption_grad = jnp.stack([lax.dynamic_index_in_dim(back, o, 1, False) for o in place], axis=0)
    return loss_sum, scale * image_sum, scale * text_sum, caption_grad.reshape(slots, width)


def solution(mesh):
    both = ("blk", "cap")
    in_specs = (P(both, None), P(both, None), P(both, None), P(), P(), P(both), P(both), P(both))
    out_specs = (P(both), P(both, None), P(both, None), P(both, None))
    return jax.shard_map(shards, mesh=mesh, in_specs=in_specs, out_specs=out_specs, check_vma=False)
```

time: 289 us -> 121 us (0.42)
  waiting for transfers between devices: 236 us -> 14.2 us
  starting transfers between devices: 17.9 us -> 86.4 us
  between operations: 15.4 us -> 2.63 us
  matrix products: 12.9 us -> 5.77 us
  other arithmetic: 2.76 us -> 8.39 us
    reduce_scatter x1 -> x0, waiting for transfers between devices: 112 us -> none  [shards(): lax.psum_scatter(jnp.dot(coeff.T, image_emb, preferred_element_type=jnp.f...]
    all_gather x1 -> x0, waiting for transfers between devices: 77 us -> none  [shards(): piece = lax.all_gather(text_emb, 'blk', axis=0, tiled=True)]
    ppermute x0 -> x18, starting transfers between devices: none -> 72.7 us  [the longest x2 16.1 us: shards(): lax.ppermute(tagged[k], 'cap', shift_zh(k))]
    all_to_all x2, waiting for transfers between devices: 46.6 us -> 3.07 us  [the longest x1 3.07 us: shards(): lax.all_to_all(back.reshape(N_Y, N_ZH * run, width), 'cap', 0, 0, axis_in...]
    ppermute x0 -> x18, waiting for transfers between devices: none -> 11.2 us  [the longest x2 7.79 us: shards(): back = lax.ppermute(tag(part, loss), 'cap', shift_zh(-k)).astype(f32)]
    dot_general x7 -> x12, matrix products: 12.9 us -> 5.77 us  [the longest x3 2.15 us: shards(): logit = scale * jnp.dot(i, e.T, preferred_element_type=f32) + bias]
    all_to_all x2, starting transfers between devices: 17.9 us -> 13.7 us  [the longest x1 6.92 us: shards(): lax.all_to_all(back.reshape(N_Y, N_ZH * run, width), 'cap', 0, 0, axis_in...]
    another operation x0 -> x3, other arithmetic: none -> 3.07 us  [the longest x1 1.03 us: shards(): jnp.stack([lax.dynamic_index_in_dim(back, o, 1, False) for o in place], a...]
  transfers between devices with their start and end apart: 4 -> 20, of which waited for: 4 -> 6; matrix products, arithmetic and copies ran while one was open for 2% -> 12% of each run, Pallas kernels for 0% -> 0%
where the time goes in v1:
time: 121 us; the launch traced here: 120 us
  starting transfers between devices  86.4 us (71%)
  waiting for transfers between devices  14.2 us (12%)
  other arithmetic  8.39 us (7%)
  matrix products  5.77 us (5%)
  between operations  2.63 us (2%)
  local copies, waits for them, and re-layouts  2.13 us (2%)
    ppermute x2, starting transfers between devices, shards(): lax.ppermute(tagged[k], 'cap', shift_zh(k))  16.1 us
    ppermute x3, starting transfers between devices, shards(): lax.ppermute(text, 'blk', shift_zl(k))  13.7 us
    ppermute x3, starting transfers between devices, shards(): lax.ppermute(image, 'blk', shift_x(k))  9.93 us
    ppermute x2, starting transfers between devices, shards(): back = lax.ppermute(tag(part, loss), 'cap', shift_zh(-k)).astype(f32)  9.19 us
    ppermute x3, starting transfers between devices, shards(): lax.ppermute(sent[k * rows:(k + 1) * rows], 'blk', shift_x(-k)).astype(f32)  9.15 us
    ppermute x2, waiting for transfers between devices, shards(): back = lax.ppermute(tag(part, loss), 'cap', shift_zh(-k)).astype(f32)  7.79 us
    ppermute x3, starting transfers between devices, shards(): text_sum += lax.ppermute(part, 'blk', shift_zl(-k)).astype(f32)  7.2 us
    all_to_all x1, starting transfers between devices, shards(): lax.all_to_all(back.reshape(N_Y, N_ZH * run, width), 'cap', 0, 0, axis_in...  6.92 us
  transfers between devices with their start and end apart: 20, of which 6 were waited for; matrix products, arithmetic and copies ran while one was open for 12% of the time, Pallas kernels for 0%

profile of v1, /device:TPU:1, one launch (start us, length us, event | category | flops | bytes accessed | tf_op | source)
XLA Modules:
  0.0 119.6 jit_solution(16430631477164160176)
XLA Ops:
  0.6 6.6 %collective-permute-start.5 = (bf16[48,1152]{1,0:T(8,128)(2,1)}, bf16[48,1152]{1,0:T(8,128)(2,1)S(1)}, u32[]{:S(2)}, u32[]{:S(2)}) collective-permute-start(bf16[48,1152]{1,0:T(8,128)(2,1)} %param.9), channel_id=1, source_target_pairs={{0,384},{24,408},{48,432},{72,456},{96,480},{120,504},{144,528},{1... | collective-permute-start | bytes 331784 | tf_op jit(solution)/shard_map/ppermute | solution.py:73
  7.3 4.0 %collective-permute-start.4 = (bf16[48,1152]{1,0:T(8,128)(2,1)}, bf16[48,1152]{1,0:T(8,128)(2,1)S(1)}, u32[]{:S(2)}, u32[]{:S(2)}) collective-permute-start(bf16[48,1152]{1,0:T(8,128)(2,1)} %param.9), channel_id=1, source_target_pairs={{0,192},{24,216},{48,240},{72,264},{96,288},{120,312},{144,336},{1... | collective-permute-start | bytes 331784 | tf_op jit(solution)/shard_map/ppermute | solution.py:73
  11.3 3.1 %collective-permute-start.6 = (bf16[48,1152]{1,0:T(8,128)(2,1)}, bf16[48,1152]{1,0:T(8,128)(2,1)S(1)}, u32[]{:S(2)}, u32[]{:S(2)}) collective-permute-start(bf16[48,1152]{1,0:T(8,128)(2,1)} %param.9), channel_id=1, source_target_pairs={{0,576},{24,600},{48,624},{72,648},{96,672},{120,696},{144,720},{1... | collective-permute-start | bytes 331784 | tf_op jit(solution)/shard_map/ppermute | solution.py:73
  14.4 4.4 %collective-permute-start.2 = (bf16[48,1152]{1,0:T(8,128)(2,1)}, bf16[48,1152]{1,0:T(8,128)(2,1)S(1)}, u32[]{:S(2)}, u32[]{:S(2)}) collective-permute-start(bf16[48,1152]{1,0:T(8,128)(2,1)} %param.8), channel_id=1, source_target_pairs={{0,144},{24,168},{48,0},{72,24},{96,48},{120,72},{144,96},{168,120... | collective-permute-start | bytes 331784 | tf_op jit(solution)/shard_map/ppermute | solution.py:75
  18.8 1.9 %collective-permute-start = (bf16[48,1152]{1,0:T(8,128)(2,1)}, bf16[48,1152]{1,0:T(8,128)(2,1)S(1)}, u32[]{:S(2)}, u32[]{:S(2)}) collective-permute-start(bf16[48,1152]{1,0:T(8,128)(2,1)} %param.8), channel_id=1, source_target_pairs={{0,48},{24,72},{48,96},{72,120},{96,144},{120,168},{144,0},{168,24... | collective-permute-start | bytes 331784 | tf_op jit(solution)/shard_map/ppermute | solution.py:75
  23.1 6.8 %all-to-all-start = ((bf16[8,48,1152]{2,1,0:T(8,128)(2,1)}), bf16[8,48,1152]{2,1,0:T(8,128)(2,1)S(1)}, u32[]{:S(2)}, u32[]{:S(2)}) async-start(bf16[8,48,1152]{2,1,0:T(8,128)(2,1)} %bitcast.6), calls=%async_computation | async-start | bytes 1769472 | tf_op jit(solution)/shard_map/all_to_all | solution.py:56
  32.1 3.6 %collective-permute-start.1 = (bf16[48,1152]{1,0:T(8,128)(2,1)S(1)}, bf16[48,1152]{1,0:T(8,128)(2,1)S(1)}, u32[]{:S(2)}, u32[]{:S(2)}) collective-permute-start(bf16[48,1152]{1,0:T(8,128)(2,1)S(1)} %copy-done), channel_id=1, source_target_pairs={{0,96},{24,120},{48,144},{72,168},{96,0},{120,24},{144,48},{168,72... | collective-permute-start | bytes 331784 | tf_op jit(solution)/shard_map/ppermute | solution.py:75
  35.8 10.6 %collective-permute-start.11 = (bf16[48,1280]{1,0:T(8,128)(2,1)}, bf16[48,1280]{1,0:T(8,128)(2,1)S(1)}, u32[]{:S(2)}, u32[]{:S(2)}) collective-permute-start(bf16[48,1280]{1,0:T(8,128)(2,1)} %get-tuple-element.28), channel_id=1, source_target_pairs={{0,8},{1,9},{2,10},{3,11},{4,12},{5,13},{6,14},{7,15},{8,16},{9,17... | collective-permute-start | bytes 368648 | tf_op jit(solution)/shard_map/ppermute | solution.py:71
  46.4 5.4 %collective-permute-start.13 = (bf16[48,1280]{1,0:T(8,128)(2,1)}, bf16[48,1280]{1,0:T(8,128)(2,1)S(1)}, u32[]{:S(2)}, u32[]{:S(2)}) collective-permute-start(bf16[48,1280]{1,0:T(8,128)(2,1)} %get-tuple-element.29), channel_id=1, source_target_pairs={{0,16},{1,17},{2,18},{3,19},{4,20},{5,21},{6,22},{7,23},{8,0},{9,1... | collective-permute-start | bytes 368648 | tf_op jit(solution)/shard_map/ppermute | solution.py:71
  52.0 5.1 %collective-permute-start.3 = (bf16[192,1152]{1,0:T(8,128)(2,1)S(1)}, bf16[192,1152]{1,0:T(8,128)(2,1)S(1)}, u32[]{:S(2)}, u32[]{:S(2)}) collective-permute-start(bf16[192,1152]{1,0:T(8,128)(2,1)S(1)} %pad_maximum_fusion.4), channel_id=1, source_target_pairs={{0,24},{24,0},{48,72},{72,48},{96,120},{120,96},{144,168},{168,144... | collective-permute-start | bytes 1327112 | tf_op jit(solution)/shard_map/ppermute | solution.py:77
  59.9 2.3 %collective-permute-start.7 = (bf16[192,1280]{1,0:T(8,128)(2,1)S(1)}, bf16[192,1280]{1,0:T(8,128)(2,1)S(1)}, u32[]{:S(2)}, u32[]{:S(2)}) collective-permute-start(bf16[192,1280]{1,0:T(8,128)(2,1)S(1)} %pad_maximum_fusion.3), channel_id=1, source_target_pairs={{0,24},{24,0},{48,72},{72,48},{96,120},{120,96},{144,168},{168,144... | collective-permute-start | bytes 1474568 | tf_op jit(solution)/shard_map/ppermute | solution.py:97
  62.7 1.9 %collective-permute-start.15 = (bf16[48,1152]{1,0:T(8,128)(2,1)S(1)}, bf16[48,1152]{1,0:T(8,128)(2,1)S(1)}, u32[]{:S(2)}, u32[]{:S(2)}) collective-permute-start(bf16[48,1152]{1,0:T(8,128)(2,1)S(1)} %get-tuple-element.25), channel_id=1, source_target_pairs={{0,576},{24,600},{48,624},{72,648},{96,672},{120,696},{144,720},{1... | collective-permute-start | bytes 331784 | tf_op jit(solution)/shard_map/ppermute | solution.py:110
  64.6 3.4 %collective-permute-start.17 = (bf16[48,1152]{1,0:T(8,128)(2,1)S(1)}, bf16[48,1152]{1,0:T(8,128)(2,1)S(1)}, u32[]{:S(2)}, u32[]{:S(2)}) collective-permute-start(bf16[48,1152]{1,0:T(8,128)(2,1)S(1)} %get-tuple-element.26), channel_id=1, source_target_pairs={{0,192},{24,216},{48,240},{72,264},{96,288},{120,312},{144,336},{1... | collective-permute-start | bytes 331784 | tf_op jit(solution)/shard_map/ppermute | solution.py:110
  68.0 1.9 %collective-permute-start.16 = (bf16[48,1152]{1,0:T(8,128)(2,1)S(1)}, bf16[48,1152]{1,0:T(8,128)(2,1)S(1)}, u32[]{:S(2)}, u32[]{:S(2)}) collective-permute-start(bf16[48,1152]{1,0:T(8,128)(2,1)S(1)} %get-tuple-element.27), channel_id=1, source_target_pairs={{0,384},{24,408},{48,432},{72,456},{96,480},{120,504},{144,528},{1... | collective-permute-start | bytes 331784 | tf_op jit(solution)/shard_map/ppermute | solution.py:110
  71.1 4.8 %collective-permute-start.8 = (bf16[48,1280]{1,0:T(8,128)(2,1)S(1)}, bf16[48,1280]{1,0:T(8,128)(2,1)S(1)}, u32[]{:S(2)}, u32[]{:S(2)}) collective-permute-start(bf16[48,1280]{1,0:T(8,128)(2,1)S(1)} %get-tuple-element.22), channel_id=1, source_target_pairs={{0,144},{24,168},{48,0},{72,24},{96,48},{120,72},{144,96},{168,120... | collective-permute-start | bytes 368648 | tf_op jit(solution)/shard_map/ppermute | solution.py:104
  76.0 1.9 %collective-permute-start.9 = (bf16[48,1280]{1,0:T(8,128)(2,1)S(1)}, bf16[48,1280]{1,0:T(8,128)(2,1)S(1)}, u32[]{:S(2)}, u32[]{:S(2)}) collective-permute-start(bf16[48,1280]{1,0:T(8,128)(2,1)S(1)} %get-tuple-element.23), channel_id=1, source_target_pairs={{0,96},{24,120},{48,144},{72,168},{96,0},{120,24},{144,48},{168,72... | collective-permute-start | bytes 368648 | tf_op jit(solution)/shard_map/ppermute | solution.py:104
  78.8 2.4 %collective-permute-start.10 = (bf16[48,1280]{1,0:T(8,128)(2,1)}, bf16[48,1280]{1,0:T(8,128)(2,1)}, u32[]{:S(2)}, u32[]{:S(2)}) collective-permute-start(bf16[48,1280]{1,0:T(8,128)(2,1)} %get-tuple-element.24), channel_id=1, source_target_pairs={{0,48},{24,72},{48,96},{72,120},{96,144},{120,168},{144,0},{168,24... | collective-permute-start | bytes 368648 | tf_op jit(solution)/shard_map/ppermute | solution.py:104
  81.2 1.9 %collective-permute-done.9 = bf16[48,1280]{1,0:T(8,128)(2,1)S(1)} collective-permute-done((bf16[48,1280]{1,0:T(8,128)(2,1)S(1)}, bf16[48,1280]{1,0:T(8,128)(2,1)S(1)}, u32[]{:S(2)}, u32[]{:S(2)}) %collective-permute-start.9) | collective-permute-done | bytes 122912 | tf_op jit(solution)/shard_map/ppermute | solution.py:104
  87.8 6.9 %all-to-all-start.1 = ((bf16[8,48,1152]{2,1,0:T(8,128)(2,1)}), bf16[8,48,1152]{2,1,0:T(8,128)(2,1)S(1)}, u32[]{:S(2)}, u32[]{:S(2)}) async-start(bf16[8,48,1152]{2,1,0:T(8,128)(2,1)} %bitcast.18), calls=%async_computation.1 | async-start | bytes 1769472 | tf_op jit(solution)/shard_map/all_to_all | solution.py:132
  95.1 2.9 %collective-permute-start.14 = (bf16[48,1280]{1,0:T(8,128)(2,1)S(1)}, bf16[48,1280]{1,0:T(8,128)(2,1)S(1)}, u32[]{:S(2)}, u32[]{:S(2)}) collective-permute-start(bf16[48,1280]{1,0:T(8,128)(2,1)S(1)} %pad_maximum_fusion.11), channel_id=1, source_target_pairs={{0,8},{1,9},{2,10},{3,11},{4,12},{5,13},{6,14},{7,15},{8,16},{9,17... | collective-permute-start | bytes 368648 | tf_op jit(solution)/shard_map/ppermute | solution.py:128
  98.2 6.3 %collective-permute-start.12 = (bf16[48,1280]{1,0:T(8,128)(2,1)S(1)}, bf16[48,1280]{1,0:T(8,128)(2,1)S(1)}, u32[]{:S(2)}, u32[]{:S(2)}) collective-permute-start(bf16[48,1280]{1,0:T(8,128)(2,1)S(1)} %pad_maximum_fusion.9), channel_id=1, source_target_pairs={{0,16},{1,17},{2,18},{3,19},{4,20},{5,21},{6,22},{7,23},{8,0},{9,1... | collective-permute-start | bytes 368648 | tf_op jit(solution)/shard_map/ppermute | solution.py:128
  105.8 1.4 %collective-permute-done.14 = bf16[48,1280]{1,0:T(8,128)(2,1)S(1)} collective-permute-done((bf16[48,1280]{1,0:T(8,128)(2,1)S(1)}, bf16[48,1280]{1,0:T(8,128)(2,1)S(1)}, u32[]{:S(2)}, u32[]{:S(2)}) %collective-permute-start.14) | collective-permute-done | bytes 122912 | tf_op jit(solution)/shard_map/ppermute | solution.py:128
  107.2 6.4 %collective-permute-done.12 = bf16[48,1280]{1,0:T(8,128)(2,1)S(1)} collective-permute-done((bf16[48,1280]{1,0:T(8,128)(2,1)S(1)}, bf16[48,1280]{1,0:T(8,128)(2,1)S(1)}, u32[]{:S(2)}, u32[]{:S(2)}) %collective-permute-start.12) | collective-permute-done | bytes 122912 | tf_op jit(solution)/shard_map/ppermute | solution.py:128
  115.4 3.1 %all-to-all-done.1 = bf16[8,48,1152]{2,1,0:T(8,128)(2,1)S(1)} async-done(((bf16[8,48,1152]{2,1,0:T(8,128)(2,1)}), bf16[8,48,1152]{2,1,0:T(8,128)(2,1)S(1)}, u32[]{:S(2)}, u32[]{:S(2)}) %all-to-all-start.1) | async-done | bytes 884768 | tf_op jit(solution)/shard_map/all_to_all | solution.py:132
  (99 shorter events, 17.7 us)
Async XLA Ops:
  0.6 56.5 %collective-permute-start.5 = (bf16[48,1152]{1,0:T(8,128)(2,1)}, bf16[48,1152]{1,0:T(8,128)(2,1)S(1)}, u32[]{:S(2)}, u32[]{:S(2)}) collective-permute-start(bf16[48,1152]{1,0:T(8,128)(2,1)} %param.9), channel_id=1, source_target_pairs={{0,384},{24,408},{48,432},{72,456},{96,480},{120,504},{144,528},{1... | collective-permute-start | bytes 331784 | tf_op jit(solution)/shard_map/ppermute | solution.py:73
  7.3 44.7 %collective-permute-start.4 = (bf16[48,1152]{1,0:T(8,128)(2,1)}, bf16[48,1152]{1,0:T(8,128)(2,1)S(1)}, u32[]{:S(2)}, u32[]{:S(2)}) collective-permute-start(bf16[48,1152]{1,0:T(8,128)(2,1)} %param.9), channel_id=1, source_target_pairs={{0,192},{24,216},{48,240},{72,264},{96,288},{120,312},{144,336},{1... | collective-permute-start | bytes 331784 | tf_op jit(solution)/shard_map/ppermute | solution.py:73
  11.3 45.9 %collective-permute-start.6 = (bf16[48,1152]{1,0:T(8,128)(2,1)}, bf16[48,1152]{1,0:T(8,128)(2,1)S(1)}, u32[]{:S(2)}, u32[]{:S(2)}) collective-permute-start(bf16[48,1152]{1,0:T(8,128)(2,1)} %param.9), channel_id=1, source_target_pairs={{0,576},{24,600},{48,624},{72,648},{96,672},{120,696},{144,720},{1... | collective-permute-start | bytes 331784 | tf_op jit(solution)/shard_map/ppermute | solution.py:73
  14.4 21.4 %collective-permute-start.2 = (bf16[48,1152]{1,0:T(8,128)(2,1)}, bf16[48,1152]{1,0:T(8,128)(2,1)S(1)}, u32[]{:S(2)}, u32[]{:S(2)}) collective-permute-start(bf16[48,1152]{1,0:T(8,128)(2,1)} %param.8), channel_id=1, source_target_pairs={{0,144},{24,168},{48,0},{72,24},{96,48},{120,72},{144,96},{168,120... | collective-permute-start | bytes 331784 | tf_op jit(solution)/shard_map/ppermute | solution.py:75
  18.8 13.3 %collective-permute-start = (bf16[48,1152]{1,0:T(8,128)(2,1)}, bf16[48,1152]{1,0:T(8,128)(2,1)S(1)}, u32[]{:S(2)}, u32[]{:S(2)}) collective-permute-start(bf16[48,1152]{1,0:T(8,128)(2,1)} %param.8), channel_id=1, source_target_pairs={{0,48},{24,72},{48,96},{72,120},{96,144},{120,168},{144,0},{168,24... | collective-permute-start | bytes 331784 | tf_op jit(solution)/shard_map/ppermute | solution.py:75
  22.0 9.3 %copy-start.6 = (s32[384]{0:T(512)S(1)}, s32[384]{0:T(512)}, u32[]{:S(2)}) copy-start(s32[384]{0:T(512)} %param.13) | copy-start | bytes 4612
  23.1 60.2 %all-to-all-start = ((bf16[8,48,1152]{2,1,0:T(8,128)(2,1)}), bf16[8,48,1152]{2,1,0:T(8,128)(2,1)S(1)}, u32[]{:S(2)}, u32[]{:S(2)}) async-start(bf16[8,48,1152]{2,1,0:T(8,128)(2,1)} %bitcast.6), calls=%async_computation | async-start | bytes 1769472 | tf_op jit(solution)/shard_map/all_to_all | solution.py:56
  32.1 14.3 %collective-permute-start.1 = (bf16[48,1152]{1,0:T(8,128)(2,1)S(1)}, bf16[48,1152]{1,0:T(8,128)(2,1)S(1)}, u32[]{:S(2)}, u32[]{:S(2)}) collective-permute-start(bf16[48,1152]{1,0:T(8,128)(2,1)S(1)} %copy-done), channel_id=1, source_target_pairs={{0,96},{24,120},{48,144},{72,168},{96,0},{120,24},{144,48},{168,72... | collective-permute-start | bytes 331784 | tf_op jit(solution)/shard_map/ppermute | solution.py:75
  35.8 48.6 %collective-permute-start.11 = (bf16[48,1280]{1,0:T(8,128)(2,1)}, bf16[48,1280]{1,0:T(8,128)(2,1)S(1)}, u32[]{:S(2)}, u32[]{:S(2)}) collective-permute-start(bf16[48,1280]{1,0:T(8,128)(2,1)} %get-tuple-element.28), channel_id=1, source_target_pairs={{0,8},{1,9},{2,10},{3,11},{4,12},{5,13},{6,14},{7,15},{8,16},{9,17... | collective-permute-start | bytes 368648 | tf_op jit(solution)/shard_map/ppermute | solution.py:71
  46.4 39.7 %collective-permute-start.13 = (bf16[48,1280]{1,0:T(8,128)(2,1)}, bf16[48,1280]{1,0:T(8,128)(2,1)S(1)}, u32[]{:S(2)}, u32[]{:S(2)}) collective-permute-start(bf16[48,1280]{1,0:T(8,128)(2,1)} %get-tuple-element.29), channel_id=1, source_target_pairs={{0,16},{1,17},{2,18},{3,19},{4,20},{5,21},{6,22},{7,23},{8,0},{9,1... | collective-permute-start | bytes 368648 | tf_op jit(solution)/shard_map/ppermute | solution.py:71
  52.0 6.5 %collective-permute-start.3 = (bf16[192,1152]{1,0:T(8,128)(2,1)S(1)}, bf16[192,1152]{1,0:T(8,128)(2,1)S(1)}, u32[]{:S(2)}, u32[]{:S(2)}) collective-permute-start(bf16[192,1152]{1,0:T(8,128)(2,1)S(1)} %pad_maximum_fusion.4), channel_id=1, source_target_pairs={{0,24},{24,0},{48,72},{72,48},{96,120},{120,96},{144,168},{168,144... | collective-permute-start | bytes 1327112 | tf_op jit(solution)/shard_map/ppermute | solution.py:77
  59.9 8.1 %collective-permute-start.7 = (bf16[192,1280]{1,0:T(8,128)(2,1)S(1)}, bf16[192,1280]{1,0:T(8,128)(2,1)S(1)}, u32[]{:S(2)}, u32[]{:S(2)}) collective-permute-start(bf16[192,1280]{1,0:T(8,128)(2,1)S(1)} %pad_maximum_fusion.3), channel_id=1, source_target_pairs={{0,24},{24,0},{48,72},{72,48},{96,120},{120,96},{144,168},{168,144... | collective-permute-start | bytes 1474568 | tf_op jit(solution)/shard_map/ppermute | solution.py:97
  62.7 8.5 %collective-permute-start.15 = (bf16[48,1152]{1,0:T(8,128)(2,1)S(1)}, bf16[48,1152]{1,0:T(8,128)(2,1)S(1)}, u32[]{:S(2)}, u32[]{:S(2)}) collective-permute-start(bf16[48,1152]{1,0:T(8,128)(2,1)S(1)} %get-tuple-element.25), channel_id=1, source_target_pairs={{0,576},{24,600},{48,624},{72,648},{96,672},{120,696},{144,720},{1... | collective-permute-start | bytes 331784 | tf_op jit(solution)/shard_map/ppermute | solution.py:110
  64.6 11.4 %collective-permute-start.17 = (bf16[48,1152]{1,0:T(8,128)(2,1)S(1)}, bf16[48,1152]{1,0:T(8,128)(2,1)S(1)}, u32[]{:S(2)}, u32[]{:S(2)}) collective-permute-start(bf16[48,1152]{1,0:T(8,128)(2,1)S(1)} %get-tuple-element.26), channel_id=1, source_target_pairs={{0,192},{24,216},{48,240},{72,264},{96,288},{120,312},{144,336},{1... | collective-permute-start | bytes 331784 | tf_op jit(solution)/shard_map/ppermute | solution.py:110
  68.0 10.0 %collective-permute-start.16 = (bf16[48,1152]{1,0:T(8,128)(2,1)S(1)}, bf16[48,1152]{1,0:T(8,128)(2,1)S(1)}, u32[]{:S(2)}, u32[]{:S(2)}) collective-permute-start(bf16[48,1152]{1,0:T(8,128)(2,1)S(1)} %get-tuple-element.27), channel_id=1, source_target_pairs={{0,384},{24,408},{48,432},{72,456},{96,480},{120,504},{144,528},{1... | collective-permute-start | bytes 331784 | tf_op jit(solution)/shard_map/ppermute | solution.py:110
  71.1 10.0 %collective-permute-start.8 = (bf16[48,1280]{1,0:T(8,128)(2,1)S(1)}, bf16[48,1280]{1,0:T(8,128)(2,1)S(1)}, u32[]{:S(2)}, u32[]{:S(2)}) collective-permute-start(bf16[48,1280]{1,0:T(8,128)(2,1)S(1)} %get-tuple-element.22), channel_id=1, source_target_pairs={{0,144},{24,168},{48,0},{72,24},{96,48},{120,72},{144,96},{168,120... | collective-permute-start | bytes 368648 | tf_op jit(solution)/shard_map/ppermute | solution.py:104
  76.0 7.1 %collective-permute-start.9 = (bf16[48,1280]{1,0:T(8,128)(2,1)S(1)}, bf16[48,1280]{1,0:T(8,128)(2,1)S(1)}, u32[]{:S(2)}, u32[]{:S(2)}) collective-permute-start(bf16[48,1280]{1,0:T(8,128)(2,1)S(1)} %get-tuple-element.23), channel_id=1, source_target_pairs={{0,96},{24,120},{48,144},{72,168},{96,0},{120,24},{144,48},{168,72... | collective-permute-start | bytes 368648 | tf_op jit(solution)/shard_map/ppermute | solution.py:104
  78.8 25.9 %collective-permute-start.10 = (bf16[48,1280]{1,0:T(8,128)(2,1)}, bf16[48,1280]{1,0:T(8,128)(2,1)}, u32[]{:S(2)}, u32[]{:S(2)}) collective-permute-start(bf16[48,1280]{1,0:T(8,128)(2,1)} %get-tuple-element.24), channel_id=1, source_target_pairs={{0,48},{24,72},{48,96},{72,120},{96,144},{120,168},{144,0},{168,24... | collective-permute-start | bytes 368648 | tf_op jit(solution)/shard_map/ppermute | solution.py:104
  86.8 11.2 %copy-start.5 = (f32[48,128]{1,0:T(8,128)S(1)}, f32[48,128]{1,0:T(8,128)}, u32[]{:S(2)}) copy-start(f32[48,128]{1,0:T(8,128)} %copy-done.4) | copy-start | bytes 73732
  87.8 30.6 %all-to-all-start.1 = ((bf16[8,48,1152]{2,1,0:T(8,128)(2,1)}), bf16[8,48,1152]{2,1,0:T(8,128)(2,1)S(1)}, u32[]{:S(2)}, u32[]{:S(2)}) async-start(bf16[8,48,1152]{2,1,0:T(8,128)(2,1)} %bitcast.18), calls=%async_computation.1 | async-start | bytes 1769472 | tf_op jit(solution)/shard_map/all_to_all | solution.py:132
  94.7 19.2 %copy-start.9 = (f32[48]{0:T(128)S(1)}, f32[48]{0:T(128)}, u32[]{:S(2)}) copy-start(f32[48]{0:T(128)} %get-tuple-element.42) | copy-start | bytes 580
  94.7 19.8 %copy-start.3 = (f32[48,128]{1,0:T(8,128)S(1)}, f32[48,128]{1,0:T(8,128)}, u32[]{:S(2)}) copy-start(f32[48,128]{1,0:T(8,128)} %copy-done.2) | copy-start | bytes 73732
  95.1 12.1 %collective-permute-start.14 = (bf16[48,1280]{1,0:T(8,128)(2,1)S(1)}, bf16[48,1280]{1,0:T(8,128)(2,1)S(1)}, u32[]{:S(2)}, u32[]{:S(2)}) collective-permute-start(bf16[48,1280]{1,0:T(8,128)(2,1)S(1)} %pad_maximum_fusion.11), channel_id=1, source_target_pairs={{0,8},{1,9},{2,10},{3,11},{4,12},{5,13},{6,14},{7,15},{8,16},{9,17... | collective-permute-start | bytes 368648 | tf_op jit(solution)/shard_map/ppermute | solution.py:128
  98.2 15.4 %collective-permute-start.12 = (bf16[48,1280]{1,0:T(8,128)(2,1)S(1)}, bf16[48,1280]{1,0:T(8,128)(2,1)S(1)}, u32[]{:S(2)}, u32[]{:S(2)}) collective-permute-start(bf16[48,1280]{1,0:T(8,128)(2,1)S(1)} %pad_maximum_fusion.9), channel_id=1, source_target_pairs={{0,16},{1,17},{2,18},{3,19},{4,20},{5,21},{6,22},{7,23},{8,0},{9,1... | collective-permute-start | bytes 368648 | tf_op jit(solution)/shard_map/ppermute | solution.py:128
  (7 other events, 45.0 us)

commit v2 on v0

v2 whole, which is shorter than its diff:
```python
import jax
import jax.numpy as jnp
from jax import lax
from jax.experimental import pallas as pl
from jax.experimental.pallas import tpu as pltpu
from jax.sharding import PartitionSpec as P

N_ZL, N_X, N_C = 4, 4, 2
N_ZH, N_Y = 3, 8
LANES = 128
LATE = 200_000_000_000
PREP, JOIN, STACK, CAPS, FOLD, FOLD2 = 0, LATE, 5_000_000_000, LATE, LATE, 0

F32, BF16 = jnp.float32, jnp.bfloat16
SMEM = pl.BlockSpec(memory_space=pltpu.SMEM)
VMEM = pl.BlockSpec(memory_space=pltpu.VMEM)
ANY = pl.BlockSpec(memory_space=pl.ANY)
HBM = pl.BlockSpec(memory_space=pltpu.HBM)


def partners(zl_bits, x_bits, c_bits):
    def blk_of(zl, x, c):
        return (zl * N_X + x) * N_C + c

    return [
        (blk_of(z, x, c), blk_of(z ^ zl_bits, x ^ x_bits, c ^ c_bits))
        for z in range(N_ZL) for x in range(N_X) for c in range(N_C)
    ]


ZL_NEAR, ZL_FAR = partners(1, 0, 0), partners(2, 0, 0)
X_NEAR, X_FAR = partners(0, 1, 0), partners(0, 3, 0)
OTHER_CORE = partners(0, 0, 1)
Y_GROUPS = [[h * N_Y + y for y in range(N_Y)] for h in range(N_ZH)]


def shift_zh(k):
    return [(h * N_Y + y, ((h + k) % N_ZH) * N_Y + y) for h in range(N_ZH) for y in range(N_Y)]


def call(body, outs, ins, in_specs, out_specs=None, scratch=(), flops=0, moved=0, room=8):
    return pl.pallas_call(
        body,
        out_shape=tuple(jax.ShapeDtypeStruct(s, d) for s, d in outs),
        in_specs=in_specs,
        out_specs=tuple(out_specs or [VMEM] * len(outs)),
        scratch_shapes=list(scratch),
        cost_estimate=pl.CostEstimate(flops=flops, bytes_accessed=moved, transcendentals=0),
        compiler_params=pltpu.CompilerParams(vmem_limit_bytes=room * 1024 * 1024),
    )(*ins)


def nt(a, b):
    return lax.dot_general(a, b, (((1,), (1,)), ((), ())), preferred_element_type=F32)


def tn(a, b):
    return lax.dot_general(a, b, (((0,), (0,)), ((), ())), preferred_element_type=F32)


def nn(a, b):
    return jnp.dot(a, b, preferred_element_type=F32)


def soft_terms(u):
    e = jnp.exp(-jnp.abs(u))
    return jnp.maximum(u, 0.0) + jnp.log1p(e), jnp.where(u >= 0, 1.0, e) / (1.0 + e)


def loss_lanes(loss):
    lane = lax.broadcasted_iota(jnp.int32, (loss.shape[0], LANES), 1)
    return jnp.where(lane == 0, loss, 0.0)


def split_lanes(extra):
    lane = lax.broadcasted_iota(jnp.int32, extra.shape, 1)
    value = jnp.sum(jnp.where(lane == 0, extra, 0.0), axis=1, keepdims=True)
    high = value.astype(BF16).astype(F32)
    return jnp.where(lane == 0, high, jnp.where(lane == 1, value - high, 0.0)).astype(BF16)


def join_lanes(extra):
    lane = lax.broadcasted_iota(jnp.int32, extra.shape, 1)
    return jnp.where(lane == 0, jnp.sum(extra, axis=1, keepdims=True), 0.0)


def prepare(zh_ref, caption, image, owner, valid, count, outgoing, tag1, tag2, own_marks,
            image_v, owner_v, valid_v, count_v, sems, more_sems):
    zh = zh_ref[0]
    rows, width = image.shape
    third = owner.shape[1] // N_ZH
    small = [
        pltpu.make_async_copy(src, dst, more_sems.at[n])
        for n, (src, dst) in enumerate(((owner, owner_v), (valid, valid_v), (count, count_v), (image, image_v)))
    ]
    copies = [
        pltpu.make_async_copy(caption.at[lax.rem(zh + (N_ZH - k), N_ZH)], outgoing.at[:, k], sems.at[k])
        for k in range(N_ZH)
    ]
    for copy in small + copies:
        copy.start()
    for copy in small:
        copy.wait()
    diagonal = lax.broadcasted_iota(jnp.int32, (rows, rows), 0) == lax.broadcasted_iota(jnp.int32, (rows, rows), 1)
    number = jnp.sum(jnp.where(diagonal, count_v[...].astype(F32), 0.0), axis=1, keepdims=True)
    number = jnp.maximum(number, 1.0)
    holds = owner_v[...] == lax.broadcasted_iota(jnp.int32, (rows, N_ZH * third), 0)
    marks = jnp.where(holds & (valid_v[...] > 0), number, 0.0).astype(BF16)
    parts = [marks[:, h * third:(h + 1) * third] for h in range(N_ZH)]
    for k, ref in enumerate((own_marks, tag1, tag2)):
        to = lax.rem(zh + k, N_ZH)
        part = jnp.where(to == 0, parts[0], jnp.where(to == 1, parts[1], parts[2]))
        if k == 0:
            ref[...] = part
        else:
            ref[:, :width] = image_v[...]
            ref[:, width:] = part
    for copy in copies:
        copy.wait()


def join(image, got_image, text, got_text, after, images, texts):
    for first, second, out in ((image, got_image, images), (text, got_text, texts)):
        rows = first.shape[0]
        out[:rows, :] = first[...]
        out[rows:, :] = second[...]


def stack(images1, images2, texts1, texts2, images, texts):
    for first, second, out in ((images1, images2, images), (texts1, texts2, texts)):
        rows = first.shape[0]
        out[:rows, :] = first[...]
        out[rows:, :] = second[...]


def pairs(scale_ref, bias_ref, near_images, far_images, texts, keep, send, keep_text, send_text, rows):
    width = texts.shape[1]
    half = texts.shape[0] // 2
    sums = None
    for images in (near_images, far_images):
        logits = scale_ref[0] * nt(images[...], texts[...]) + bias_ref[0]
        if images is near_images:
            left = lax.broadcasted_iota(jnp.int32, logits.shape, 0)
            right = lax.broadcasted_iota(jnp.int32, logits.shape, 1)
            match = (left == right) & (left < rows)
            loss, slope = soft_terms(jnp.where(match, -logits, logits))
            coeff = jnp.where(match, -slope, slope).astype(BF16)
        else:
            loss, slope = soft_terms(logits)
            coeff = slope.astype(BF16)
        extra = loss_lanes(jnp.sum(loss, axis=1, keepdims=True))
        grad = nn(coeff, texts[...])
        more = tn(coeff, images[...])
        if images is near_images:
            keep[:, :width] = grad
            keep[:, width:] = extra
            sums = more
        else:
            send[:, :width] = grad.astype(BF16)
            send[:, width:] = split_lanes(extra)
            sums = sums + more
    keep_text[...] = sums[:half]
    send_text[...] = sums[half:].astype(BF16)


def fold_tagged(own, got, keep, send):
    half, width = keep.shape[0], keep.shape[1] - LANES
    for ref, rows in ((keep, slice(0, half)), (send, slice(half, 2 * half))):
        ref[:, :width] = (own[rows, :width] + got[rows, :width].astype(F32)).astype(ref.dtype)
        extra = own[rows, width:] + join_lanes(got[rows, width:].astype(F32))
        ref[:, width:] = extra if ref is keep else split_lanes(extra)


def fold_last(scale_ref, own, got, own_text, got_text, keep, send, text_grad):
    fold_tagged(own, got, keep, send)
    text_grad[...] = scale_ref[0] * (own_text[...] + got_text[...].astype(F32))


def fold_both(own, got, own_text, got_text, keep, send, keep_text, send_text):
    fold_tagged(own, got, keep, send)
    half = keep_text.shape[0]
    keep_text[...] = own_text[:half, :] + got_text[:half, :].astype(F32)
    send_text[...] = (own_text[half:, :] + got_text[half:, :].astype(F32)).astype(BF16)


def captions(scale_ref, bias_ref, arrived, image, own_marks, tag1, tag2, back, own, send1, send2,
             here, done, in_sems, out_sems):
    width = image.shape[1]
    slots = arrived.shape[0] * arrived.shape[2]
    scale, bias = scale_ref[0], bias_ref[0]
    loads = [pltpu.make_async_copy(arrived.at[:, k], here.at[k], in_sems.at[k]) for k in range(N_ZH)]
    stores = [pltpu.make_async_copy(done.at[k], back.at[:, k], out_sems.at[k]) for k in range(N_ZH)]
    for load in loads:
        load.start()
    for k in range(N_ZH):
        if k == 0:
            i, mark = image[...], own_marks[...].astype(F32)
        else:
            ref = (tag1, tag2)[k - 1]
            i, mark = ref[:, :width], ref[:, width:].astype(F32)
        loads[k].wait()
        e = here[k].reshape(slots, width)
        there = mark > 0
        denom = jnp.where(there, mark, 1.0)
        loss, slope = soft_terms(-(scale * nt(i, e) + bias))
        loss = jnp.sum(jnp.where(there, loss / denom, 0.0), axis=1, keepdims=True)
        weight = jnp.where(there, -slope / denom, 0.0).astype(BF16)
        done[k] = (scale * tn(weight, i)).astype(BF16).reshape(done.shape[1:])
        stores[k].start()
        part = nn(weight, e)
        if k == 0:
            own[:, :width] = part
            own[:, width:] = loss_lanes(loss)
        else:
            ref = (send1, send2)[k - 1]
            ref[:, :width] = part.astype(BF16)
            ref[:, width:] = split_lanes(loss_lanes(loss))
    for store in stores:
        store.wait()


def finish(scale_ref, own, got, cap_own, cap1, cap2, loss, image_grad):
    rows, width = image_grad.shape
    total = own[...] + got[...].astype(F32) + cap_own[...] + cap1[...].astype(F32) + cap2[...].astype(F32)
    image_grad[...] = scale_ref[0] * total[:, :width]
    column = jnp.sum(total[:, width:], axis=1, keepdims=True)
    diagonal = lax.broadcasted_iota(jnp.int32, (rows, rows), 0) == lax.broadcasted_iota(jnp.int32, (rows, rows), 1)
    loss[...] = jnp.sum(jnp.where(diagonal, column, 0.0), axis=0, keepdims=True)


def place(zh_ref, back, out, here, in_sems, out_sems):
    zh = zh_ref[0]
    loads = [pltpu.make_async_copy(back.at[:, k], here.at[k], in_sems.at[k]) for k in range(N_ZH)]
    stores = [
        pltpu.make_async_copy(here.at[k], out.at[lax.rem(zh + (N_ZH - k), N_ZH)], out_sems.at[k])
        for k in range(N_ZH)
    ]
    for load in loads:
        load.start()
    for load, store in zip(loads, stores):
        load.wait()
        store.start()
    for store in stores:
        store.wait()


def shards(image, text, caption, logit_scale, logit_bias, owner, valid, count):
    rows, width = image.shape
    wide = width + LANES
    slots = caption.shape[0]
    run = slots // (N_ZH * N_Y)
    third = slots // N_ZH
    zh = (lax.axis_index("cap") // N_Y).astype(jnp.int32).reshape(1)
    sems = pltpu.SemaphoreType.DMA((N_ZH,))

    outgoing, tag1, tag2, own_marks = call(
        prepare,
        [((N_Y, N_ZH, run, width), BF16), ((rows, wide), BF16), ((rows, wide), BF16), ((rows, third), BF16)],
        (zh, caption.reshape(N_ZH, N_Y, run, width), image, owner.reshape(1, slots), valid.reshape(1, slots),
         count.reshape(1, rows)),
        [SMEM] + [HBM] * 5, [VMEM] * 4,
        [pltpu.VMEM((rows, width), BF16), pltpu.VMEM((1, slots), jnp.int32), pltpu.VMEM((1, slots), jnp.int32),
         pltpu.VMEM((1, rows), jnp.int32), sems, pltpu.SemaphoreType.DMA((4,))],
        flops=PREP, room=8,
    )

    def to_y(x):
        x = x.reshape(N_Y, N_ZH * run, width)
        x = lax.all_to_all(x, "cap", 0, 0, axis_index_groups=Y_GROUPS, tiled=True)
        return x.reshape(N_Y, N_ZH, run, width)

    arrived = to_y(outgoing)
    from1 = lax.ppermute(tag1, "cap", shift_zh(1))
    from2 = lax.ppermute(tag2, "cap", shift_zh(2))

    images, texts = call(
        join, [((2 * rows, width), BF16)] * 2,
        (image, lax.ppermute(image, "blk", X_FAR), text, lax.ppermute(text, "blk", ZL_FAR), tag1),
        [VMEM] * 4 + [ANY], flops=JOIN,
    )
    images, texts = call(
        stack, [((4 * rows, width), BF16)] * 2,
        (images, lax.ppermute(images, "blk", X_NEAR), texts, lax.ppermute(texts, "blk", ZL_NEAR)), [VMEM] * 4,
        flops=STACK,
    )
    others = lax.ppermute(images, "blk", OTHER_CORE)
    n_i, n_t = 2 * N_X * rows, N_ZL * rows
    keep, send, keep_t, send_t = call(
        lambda *refs: pairs(*refs, rows=rows),
        [((n_i // 2, wide), F32), ((n_i // 2, wide), BF16), ((n_t // 2, width), F32), ((n_t // 2, width), BF16)],
        (logit_scale, logit_bias, images, others, texts), [SMEM, SMEM] + [VMEM] * 3,
        flops=6 * n_i * n_t * width, moved=8 * n_i * width,
    )
    got = lax.ppermute(send, "blk", OTHER_CORE)
    got_t = lax.ppermute(send_t, "blk", ZL_NEAR)

    back, cap_own, send1, send2 = call(
        captions,
        [((N_Y, N_ZH, run, width), BF16), ((rows, wide), F32), ((rows, wide), BF16), ((rows, wide), BF16)],
        (logit_scale, logit_bias, arrived, image, own_marks, from1, from2), [SMEM, SMEM, ANY] + [VMEM] * 4,
        [ANY] + [VMEM] * 3, [pltpu.VMEM((N_ZH, N_Y, run, width), BF16)] * 2 + [sems, sems], flops=CAPS,
    )
    returned = to_y(back)
    cap1 = lax.ppermute(send1, "cap", shift_zh(-1))
    cap2 = lax.ppermute(send2, "cap", shift_zh(-2))

    keep, send, keep_t, send_t = call(
        fold_both,
        [((n_i // 4, wide), F32), ((n_i // 4, wide), BF16), ((rows, width), F32), ((rows, width), BF16)],
        (keep, got, keep_t, got_t), [VMEM] * 4, flops=FOLD,
    )
    got = lax.ppermute(send, "blk", X_NEAR)
    got_t = lax.ppermute(send_t, "blk", ZL_FAR)
    keep, send, text_grad = call(
        fold_last, [((rows, wide), F32), ((rows, wide), BF16), ((rows, width), F32)],
        (logit_scale, keep, got, keep_t, got_t), [SMEM] + [VMEM] * 4, flops=FOLD2,
    )
    got = lax.ppermute(send, "blk", X_FAR)
    loss, image_grad = call(
        finish, [((1, rows), F32), ((rows, width), F32)],
        (logit_scale, keep, got, cap_own, cap1, cap2), [SMEM] + [VMEM] * 5, moved=rows * wide * 20,
    )
    (caption_grad,) = call(
        place, [((N_ZH, N_Y, run, width), BF16)], (zh, returned), [SMEM, ANY], [ANY],
        [pltpu.VMEM((N_ZH, N_Y, run, width), BF16), sems, sems], moved=4 * slots * width
    )
    return loss.reshape(rows), image_grad, text_grad, caption_grad.reshape(slots, width)


def solution(mesh):
    both = ("blk", "cap")
    in_specs = (P(both, None), P(both, None), P(both, None), P(), P(), P(both), P(both), P(both))
    out_specs = (P(both), P(both, None), P(both, None), P(both, None))
    return jax.shard_map(shards, mesh=mesh, in_specs=in_specs, out_specs=out_specs, check_vma=False)
```

time: 289 us -> 114 us (0.39)
  waiting for transfers between devices: 236 us -> 23.4 us
  starting transfers between devices: 17.9 us -> 70.4 us
  between operations: 15.4 us -> 2.19 us
  matrix products: 12.9 us -> 0 us
  Pallas kernels: 0 us -> 12.5 us
  local copies, waits for them, and re-layouts: 0.94 us -> 4.08 us
    reduce_scatter x1 -> x0, waiting for transfers between devices: 112 us -> none  [shards(): lax.psum_scatter(jnp.dot(coeff.T, image_emb, preferred_element_type=jnp.f...]
    all_gather x1 -> x0, waiting for transfers between devices: 77 us -> none  [shards(): piece = lax.all_gather(text_emb, 'blk', axis=0, tiled=True)]
    ppermute x0 -> x14, starting transfers between devices: none -> 56.7 us  [the longest x1 10.3 us: shards(): from1 = lax.ppermute(tag1, 'cap', shift_zh(1))]
    all_to_all x2, waiting for transfers between devices: 46.6 us -> 0.01 us  [to_y(): x = lax.all_to_all(x, 'cap', 0, 0, axis_index_groups=Y_GROUPS, tiled=True)]
    ppermute x0 -> x14, waiting for transfers between devices: none -> 23.4 us  [the longest x1 6.32 us: shards(): from2 = lax.ppermute(tag2, 'cap', shift_zh(2))]
    dot_general x7 -> x0, matrix products: 12.9 us -> none  [the longest x1 4.12 us: shards(): jnp.dot(coeff.T, image_emb, preferred_element_type=jnp.float32)]
    pallas_call x0 -> x9, Pallas kernels: none -> 12.5 us  [call(): pl.pallas_call(body, out_shape=tuple((jax.ShapeDtypeStruct(s, d) for s, d...]
    all_to_all x2, starting transfers between devices: 17.9 us -> 13.6 us  [to_y(): x = lax.all_to_all(x, 'cap', 0, 0, axis_index_groups=Y_GROUPS, tiled=True)]
  transfers between devices with their start and end apart: 4 -> 16, of which waited for: 4 -> 6; matrix products, arithmetic and copies ran while one was open for 2% -> 0% of each run, Pallas kernels for 0% -> 9%
where the time goes in v2:
time: 114 us; the launch traced here: 113 us
  starting transfers between devices  70.4 us (62%)
  waiting for transfers between devices  23.4 us (21%)
  Pallas kernels  12.5 us (11%)
  local copies, waits for them, and re-layouts  4.08 us (4%)
  between operations  2.19 us (2%)
    all_to_all x2, starting transfers between devices, to_y(): x = lax.all_to_all(x, 'cap', 0, 0, axis_index_groups=Y_GROUPS, tiled=True)  13.6 us
    pallas_call x9, Pallas kernels, call(): pl.pallas_call(body, out_shape=tuple((jax.ShapeDtypeStruct(s, d) for s, d...  12.5 us
    ppermute x1, starting transfers between devices, shards(): from1 = lax.ppermute(tag1, 'cap', shift_zh(1))  10.3 us
    ppermute x1, waiting for transfers between devices, shards(): from2 = lax.ppermute(tag2, 'cap', shift_zh(2))  6.32 us
    ppermute x1, starting transfers between devices, shards(): lax.ppermute(text, 'blk', ZL_FAR)  5.81 us
    ppermute x1, waiting for transfers between devices, shards(): cap1 = lax.ppermute(send1, 'cap', shift_zh(-1))  5.47 us
    ppermute x1, starting transfers between devices, shards(): lax.ppermute(image, 'blk', X_FAR)  5.22 us
    ppermute x1, starting transfers between devices, shards(): cap2 = lax.ppermute(send2, 'cap', shift_zh(-2))  5.22 us
  transfers between devices with their start and end apart: 16, of which 6 were waited for; matrix products, arithmetic and copies ran while one was open for 0% of the time, Pallas kernels for 9%

profile of v2, /device:TPU:1, one launch (start us, length us, event | category | flops | bytes accessed | tf_op | source)
XLA Modules:
  0.0 112.5 jit_solution(16407533954731820468)
XLA Ops:
  0.6 5.2 %collective-permute-start = (bf16[48,1152]{1,0:T(8,128)(2,1)}, bf16[48,1152]{1,0:T(8,128)(2,1)S(1)}, u32[]{:S(2)}, u32[]{:S(2)}) collective-permute-start(bf16[48,1152]{1,0:T(8,128)(2,1)} %image.5), channel_id=1, source_target_pairs={{0,144},{24,168},{48,96},{72,120},{96,48},{120,72},{144,0},{168,24... | collective-permute-start | bytes 331784 | tf_op jit(solution)/shard_map/ppermute | solution.py:278
  5.9 5.8 %collective-permute-start.1 = (bf16[48,1152]{1,0:T(8,128)(2,1)}, bf16[48,1152]{1,0:T(8,128)(2,1)S(1)}, u32[]{:S(2)}, u32[]{:S(2)}) collective-permute-start(bf16[48,1152]{1,0:T(8,128)(2,1)} %text.1), channel_id=1, source_target_pairs={{0,384},{24,408},{48,432},{72,456},{96,480},{120,504},{144,528},{1... | collective-permute-start | bytes 331784 | tf_op jit(solution)/shard_map/ppermute | solution.py:278
  17.1 7.0 %all-to-all-start = ((bf16[8,48,1152]{2,1,0:T(8,128)(2,1)}), bf16[8,48,1152]{2,1,0:T(8,128)(2,1)}, u32[]{:S(2)}, u32[]{:S(2)}) async-start(bf16[8,48,1152]{2,1,0:T(8,128)(2,1)} %bitcast.3), calls=%async_computation | async-start | bytes 1769472 | tf_op jit(solution)/shard_map/all_to_all | solution.py:269
  24.2 1.9 %collective-permute-start.2 = (bf16[96,1152]{1,0:T(8,128)(2,1)S(1)}, bf16[96,1152]{1,0:T(8,128)(2,1)S(1)}, u32[]{:S(2)}, u32[]{:S(2)}) collective-permute-start(bf16[96,1152]{1,0:T(8,128)(2,1)S(1)} %get-tuple-element.30.images1), channel_id=1, source_target_pairs={{0,48},{24,72},{48,0},{72,24},{96,144},{120,168},{144,96},{168,120... | collective-permute-start | bytes 663560 | tf_op jit(solution)/shard_map/ppermute | solution.py:283
  26.1 4.0 %collective-permute-start.3 = (bf16[96,1152]{1,0:T(8,128)(2,1)S(1)}, bf16[96,1152]{1,0:T(8,128)(2,1)S(1)}, u32[]{:S(2)}, u32[]{:S(2)}) collective-permute-start(bf16[96,1152]{1,0:T(8,128)(2,1)S(1)} %get-tuple-element.31.texts1), channel_id=1, source_target_pairs={{0,192},{24,216},{48,240},{72,264},{96,288},{120,312},{144,336},{1... | collective-permute-start | bytes 663560 | tf_op jit(solution)/shard_map/ppermute | solution.py:283
  31.6 2.6 %collective-permute-done.3.texts2 = bf16[96,1152]{1,0:T(8,128)(2,1)S(1)} collective-permute-done((bf16[96,1152]{1,0:T(8,128)(2,1)S(1)}, bf16[96,1152]{1,0:T(8,128)(2,1)S(1)}, u32[]{:S(2)}, u32[]{:S(2)}) %collective-permute-start.3) | collective-permute-done | bytes 221216 | tf_op jit(solution)/shard_map/ppermute | solution.py:283
  34.3 4.2 %collective-permute-start.4 = (bf16[192,1152]{1,0:T(8,128)(2,1)S(1)}, bf16[192,1152]{1,0:T(8,128)(2,1)S(1)}, u32[]{:S(2)}, u32[]{:S(2)}) collective-permute-start(bf16[192,1152]{1,0:T(8,128)(2,1)S(1)} %get-tuple-element.32.refs_2_), channel_id=1, source_target_pairs={{0,24},{24,0},{48,72},{72,48},{96,120},{120,96},{144,168},{168,144... | collective-permute-start | bytes 1327112 | tf_op jit(solution)/shard_map/ppermute | solution.py:286
  38.4 10.3 %collective-permute-start.10 = (bf16[48,1280]{1,0:T(8,128)(2,1)S(1)}, bf16[48,1280]{1,0:T(8,128)(2,1)S(1)}, u32[]{:S(2)}, u32[]{:S(2)}) collective-permute-start(bf16[48,1280]{1,0:T(8,128)(2,1)S(1)} %get-tuple-element.29.after), channel_id=1, source_target_pairs={{0,8},{1,9},{2,10},{3,11},{4,12},{5,13},{6,14},{7,15},{8,16},{9,17... | collective-permute-start | bytes 368648 | tf_op jit(solution)/shard_map/ppermute | solution.py:273
  48.8 3.4 %collective-permute-start.11 = (bf16[48,1280]{1,0:T(8,128)(2,1)S(1)}, bf16[48,1280]{1,0:T(8,128)(2,1)S(1)}, u32[]{:S(2)}, u32[]{:S(2)}) collective-permute-start(bf16[48,1280]{1,0:T(8,128)(2,1)S(1)} %get-tuple-element.46), channel_id=1, source_target_pairs={{0,16},{1,17},{2,18},{3,19},{4,20},{5,21},{6,22},{7,23},{8,0},{9,1... | collective-permute-start | bytes 368648 | tf_op jit(solution)/shard_map/ppermute | solution.py:274
  53.5 2.4 %shard_map.114 = (f32[192,1280]{1,0:T(8,128)S(1)}, bf16[192,1280]{1,0:T(8,128)(2,1)}, f32[96,1152]{1,0:T(8,128)S(1)}, bf16[96,1152]{1,0:T(8,128)(2,1)}) custom-call(f32[1]{0:T(128)S(6)} %copy.12.refs_0_.scale_ref, f32[1]{0:T(128)S(6)} %copy.13.refs_1_.bias_ref, bf16[192,1152]{1,0:T(8,128)(2,1)S(1)} %get-tuple-element.32.refs_2_, ...), custom_call_target="tpu_custom_call" | custom-call | flops 509607936 | bytes 3538944 | tf_op jit(solution)/shard_map/pallas_call | solution.py:42
  55.9 2.2 %collective-permute-start.5 = (bf16[192,1280]{1,0:T(8,128)(2,1)}, bf16[192,1280]{1,0:T(8,128)(2,1)}, u32[]{:S(2)}, u32[]{:S(2)}) collective-permute-start(bf16[192,1280]{1,0:T(8,128)(2,1)} %get-tuple-element.35), channel_id=1, source_target_pairs={{0,24},{24,0},{48,72},{72,48},{96,120},{120,96},{144,168},{168,144... | collective-permute-start | bytes 1474568 | tf_op jit(solution)/shard_map/ppermute | solution.py:294
  58.1 3.1 %collective-permute-start.6 = (bf16[96,1152]{1,0:T(8,128)(2,1)}, bf16[96,1152]{1,0:T(8,128)(2,1)}, u32[]{:S(2)}, u32[]{:S(2)}) collective-permute-start(bf16[96,1152]{1,0:T(8,128)(2,1)} %get-tuple-element.37), channel_id=1, source_target_pairs={{0,192},{24,216},{48,240},{72,264},{96,288},{120,312},{144,336},{1... | collective-permute-start | bytes 663560 | tf_op jit(solution)/shard_map/ppermute | solution.py:295
  61.2 6.3 %collective-permute-done.11.tag2 = bf16[48,1280]{1,0:T(8,128)(2,1)S(1)} collective-permute-done((bf16[48,1280]{1,0:T(8,128)(2,1)S(1)}, bf16[48,1280]{1,0:T(8,128)(2,1)S(1)}, u32[]{:S(2)}, u32[]{:S(2)}) %collective-permute-start.11) | collective-permute-done | bytes 122912 | tf_op jit(solution)/shard_map/ppermute | solution.py:274
  67.5 3.7 %shard_map.117 = (bf16[8,3,16,1152]{3,2,1,0:T(8,128)(2,1)}, f32[48,1280]{1,0:T(8,128)S(1)}, bf16[48,1280]{1,0:T(8,128)(2,1)S(1)}, bf16[48,1280]{1,0:T(8,128)(2,1)S(1)}) custom-call(f32[1]{0:T(128)S(6)} %copy.12.refs_0_.scale_ref, f32[1]{0:T(128)S(6)} %copy.13.refs_1_.bias_ref, bf16[8,3,16,1152]{3,2,1,0:T(8,128)(2,1)} %bitcast.4.arrived, ...), custom_call_target="tpu_custom_call" | custom-call | flops 199999995904 | tf_op jit(solution)/shard_map/pallas_call | solution.py:42
  71.3 6.6 %all-to-all-start.1 = ((bf16[8,48,1152]{2,1,0:T(8,128)(2,1)}), bf16[8,48,1152]{2,1,0:T(8,128)(2,1)}, u32[]{:S(2)}, u32[]{:S(2)}) async-start(bf16[8,48,1152]{2,1,0:T(8,128)(2,1)} %bitcast.6), calls=%async_computation.1 | async-start | bytes 1769472 | tf_op jit(solution)/shard_map/all_to_all | solution.py:269
  79.4 3.4 %collective-permute-start.7 = (bf16[96,1280]{1,0:T(8,128)(2,1)S(1)}, bf16[96,1280]{1,0:T(8,128)(2,1)S(1)}, u32[]{:S(2)}, u32[]{:S(2)}) collective-permute-start(bf16[96,1280]{1,0:T(8,128)(2,1)S(1)} %get-tuple-element.39), channel_id=1, source_target_pairs={{0,48},{24,72},{48,0},{72,24},{96,144},{120,168},{144,96},{168,120... | collective-permute-start | bytes 737288 | tf_op jit(solution)/shard_map/ppermute | solution.py:312
  82.8 1.9 %collective-permute-start.8 = (bf16[48,1152]{1,0:T(8,128)(2,1)S(1)}, bf16[48,1152]{1,0:T(8,128)(2,1)S(1)}, u32[]{:S(2)}, u32[]{:S(2)}) collective-permute-start(bf16[48,1152]{1,0:T(8,128)(2,1)S(1)} %get-tuple-element.41), channel_id=1, source_target_pairs={{0,384},{24,408},{48,432},{72,456},{96,480},{120,504},{144,528},{1... | collective-permute-start | bytes 331784 | tf_op jit(solution)/shard_map/ppermute | solution.py:313
  84.7 5.1 %collective-permute-done.8.got_text = bf16[48,1152]{1,0:T(8,128)(2,1)S(1)} collective-permute-done((bf16[48,1152]{1,0:T(8,128)(2,1)S(1)}, bf16[48,1152]{1,0:T(8,128)(2,1)S(1)}, u32[]{:S(2)}, u32[]{:S(2)}) %collective-permute-start.8) | collective-permute-done | bytes 110624 | tf_op jit(solution)/shard_map/ppermute | solution.py:313
  90.6 2.1 %collective-permute-start.9 = (bf16[48,1280]{1,0:T(8,128)(2,1)S(1)}, bf16[48,1280]{1,0:T(8,128)(2,1)S(1)}, u32[]{:S(2)}, u32[]{:S(2)}) collective-permute-start(bf16[48,1280]{1,0:T(8,128)(2,1)S(1)} %get-tuple-element.43), channel_id=1, source_target_pairs={{0,144},{24,168},{48,96},{72,120},{96,48},{120,72},{144,0},{168,24... | collective-permute-start | bytes 368648 | tf_op jit(solution)/shard_map/ppermute | solution.py:318
  92.7 4.0 %collective-permute-start.12 = (bf16[48,1280]{1,0:T(8,128)(2,1)S(1)}, bf16[48,1280]{1,0:T(8,128)(2,1)S(1)}, u32[]{:S(2)}, u32[]{:S(2)}) collective-permute-start(bf16[48,1280]{1,0:T(8,128)(2,1)S(1)} %get-tuple-element.48), channel_id=1, source_target_pairs={{0,16},{1,17},{2,18},{3,19},{4,20},{5,21},{6,22},{7,23},{8,0},{9,1... | collective-permute-start | bytes 368648 | tf_op jit(solution)/shard_map/ppermute | solution.py:304
  96.7 5.2 %collective-permute-start.13 = (bf16[48,1280]{1,0:T(8,128)(2,1)S(1)}, bf16[48,1280]{1,0:T(8,128)(2,1)S(1)}, u32[]{:S(2)}, u32[]{:S(2)}) collective-permute-start(bf16[48,1280]{1,0:T(8,128)(2,1)S(1)} %get-tuple-element.49), channel_id=1, source_target_pairs={{0,8},{1,9},{2,10},{3,11},{4,12},{5,13},{6,14},{7,15},{8,16},{9,17... | collective-permute-start | bytes 368648 | tf_op jit(solution)/shard_map/ppermute | solution.py:305
  101.9 5.5 %collective-permute-done.12.cap1 = bf16[48,1280]{1,0:T(8,128)(2,1)S(1)} collective-permute-done((bf16[48,1280]{1,0:T(8,128)(2,1)S(1)}, bf16[48,1280]{1,0:T(8,128)(2,1)S(1)}, u32[]{:S(2)}, u32[]{:S(2)}) %collective-permute-start.12) | collective-permute-done | bytes 122912 | tf_op jit(solution)/shard_map/ppermute | solution.py:304
  107.4 2.4 %collective-permute-done.13.cap2 = bf16[48,1280]{1,0:T(8,128)(2,1)S(1)} collective-permute-done((bf16[48,1280]{1,0:T(8,128)(2,1)S(1)}, bf16[48,1280]{1,0:T(8,128)(2,1)S(1)}, u32[]{:S(2)}, u32[]{:S(2)}) %collective-permute-start.13) | collective-permute-done | bytes 122912 | tf_op jit(solution)/shard_map/ppermute | solution.py:305
  110.6 1.9 %shard_map.119 = bf16[3,8,16,1152]{3,2,1,0:T(8,128)(2,1)} custom-call(s32[1]{0:T(128)} %bitcast.zh_ref, bf16[8,3,16,1152]{3,2,1,0:T(8,128)(2,1)} %bitcast.7.back), custom_call_target="tpu_custom_call" | custom-call | bytes 1769472 | tf_op jit(solution)/shard_map/pallas_call | solution.py:42
  (33 shorter events, 10.0 us)
Async XLA Ops:
  0.6 23.4 %collective-permute-start = (bf16[48,1152]{1,0:T(8,128)(2,1)}, bf16[48,1152]{1,0:T(8,128)(2,1)S(1)}, u32[]{:S(2)}, u32[]{:S(2)}) collective-permute-start(bf16[48,1152]{1,0:T(8,128)(2,1)} %image.5), channel_id=1, source_target_pairs={{0,144},{24,168},{48,96},{72,120},{96,48},{120,72},{144,0},{168,24... | collective-permute-start | bytes 331784 | tf_op jit(solution)/shard_map/ppermute | solution.py:278
  5.9 18.2 %collective-permute-start.1 = (bf16[48,1152]{1,0:T(8,128)(2,1)}, bf16[48,1152]{1,0:T(8,128)(2,1)S(1)}, u32[]{:S(2)}, u32[]{:S(2)}) collective-permute-start(bf16[48,1152]{1,0:T(8,128)(2,1)} %text.1), channel_id=1, source_target_pairs={{0,384},{24,408},{48,432},{72,456},{96,480},{120,504},{144,528},{1... | collective-permute-start | bytes 331784 | tf_op jit(solution)/shard_map/ppermute | solution.py:278
  11.7 0.7 copy-start.5
  12.4 0.7 copy-start.6
  13.1 0.7 copy-start.3
  13.7 1.2 %copy-start = (bf16[384,1152]{1,0:T(8,128)(2,1)S(1)}, bf16[384,1152]{1,0:T(8,128)(2,1)}, u32[]{:S(2)}) copy-start(bf16[384,1152]{1,0:T(8,128)(2,1)} %param.10) | copy-start | bytes 2654212
  14.9 0.9 copy-start.1
  17.1 7.0 %copy-start.2 = (bf16[48,1152]{1,0:T(8,128)(2,1)S(1)}, bf16[48,1152]{1,0:T(8,128)(2,1)}, u32[]{:S(2)}) copy-start(bf16[48,1152]{1,0:T(8,128)(2,1)} %image.5) | copy-start | bytes 331780
  17.1 7.0 %copy-start.4 = (bf16[48,1152]{1,0:T(8,128)(2,1)S(1)}, bf16[48,1152]{1,0:T(8,128)(2,1)}, u32[]{:S(2)}) copy-start(bf16[48,1152]{1,0:T(8,128)(2,1)} %text.1) | copy-start | bytes 331780
  17.1 50.4 %all-to-all-start = ((bf16[8,48,1152]{2,1,0:T(8,128)(2,1)}), bf16[8,48,1152]{2,1,0:T(8,128)(2,1)}, u32[]{:S(2)}, u32[]{:S(2)}) async-start(bf16[8,48,1152]{2,1,0:T(8,128)(2,1)} %bitcast.3), calls=%async_computation | async-start | bytes 1769472 | tf_op jit(solution)/shard_map/all_to_all | solution.py:269
  24.2 7.4 %collective-permute-start.2 = (bf16[96,1152]{1,0:T(8,128)(2,1)S(1)}, bf16[96,1152]{1,0:T(8,128)(2,1)S(1)}, u32[]{:S(2)}, u32[]{:S(2)}) collective-permute-start(bf16[96,1152]{1,0:T(8,128)(2,1)S(1)} %get-tuple-element.30.images1), channel_id=1, source_target_pairs={{0,48},{24,72},{48,0},{72,24},{96,144},{120,168},{144,96},{168,120... | collective-permute-start | bytes 663560 | tf_op jit(solution)/shard_map/ppermute | solution.py:283
  26.1 8.1 %collective-permute-start.3 = (bf16[96,1152]{1,0:T(8,128)(2,1)S(1)}, bf16[96,1152]{1,0:T(8,128)(2,1)S(1)}, u32[]{:S(2)}, u32[]{:S(2)}) collective-permute-start(bf16[96,1152]{1,0:T(8,128)(2,1)S(1)} %get-tuple-element.31.texts1), channel_id=1, source_target_pairs={{0,192},{24,216},{48,240},{72,264},{96,288},{120,312},{144,336},{1... | collective-permute-start | bytes 663560 | tf_op jit(solution)/shard_map/ppermute | solution.py:283
  34.3 19.3 %collective-permute-start.4 = (bf16[192,1152]{1,0:T(8,128)(2,1)S(1)}, bf16[192,1152]{1,0:T(8,128)(2,1)S(1)}, u32[]{:S(2)}, u32[]{:S(2)}) collective-permute-start(bf16[192,1152]{1,0:T(8,128)(2,1)S(1)} %get-tuple-element.32.refs_2_), channel_id=1, source_target_pairs={{0,24},{24,0},{48,72},{72,48},{96,120},{120,96},{144,168},{168,144... | collective-permute-start | bytes 1327112 | tf_op jit(solution)/shard_map/ppermute | solution.py:286
  38.4 22.8 %collective-permute-start.10 = (bf16[48,1280]{1,0:T(8,128)(2,1)S(1)}, bf16[48,1280]{1,0:T(8,128)(2,1)S(1)}, u32[]{:S(2)}, u32[]{:S(2)}) collective-permute-start(bf16[48,1280]{1,0:T(8,128)(2,1)S(1)} %get-tuple-element.29.after), channel_id=1, source_target_pairs={{0,8},{1,9},{2,10},{3,11},{4,12},{5,13},{6,14},{7,15},{8,16},{9,17... | collective-permute-start | bytes 368648 | tf_op jit(solution)/shard_map/ppermute | solution.py:273
  48.8 18.7 %collective-permute-start.11 = (bf16[48,1280]{1,0:T(8,128)(2,1)S(1)}, bf16[48,1280]{1,0:T(8,128)(2,1)S(1)}, u32[]{:S(2)}, u32[]{:S(2)}) collective-permute-start(bf16[48,1280]{1,0:T(8,128)(2,1)S(1)} %get-tuple-element.46), channel_id=1, source_target_pairs={{0,16},{1,17},{2,18},{3,19},{4,20},{5,21},{6,22},{7,23},{8,0},{9,1... | collective-permute-start | bytes 368648 | tf_op jit(solution)/shard_map/ppermute | solution.py:274
  55.9 22.1 %collective-permute-start.5 = (bf16[192,1280]{1,0:T(8,128)(2,1)}, bf16[192,1280]{1,0:T(8,128)(2,1)}, u32[]{:S(2)}, u32[]{:S(2)}) collective-permute-start(bf16[192,1280]{1,0:T(8,128)(2,1)} %get-tuple-element.35), channel_id=1, source_target_pairs={{0,24},{24,0},{48,72},{72,48},{96,120},{120,96},{144,168},{168,144... | collective-permute-start | bytes 1474568 | tf_op jit(solution)/shard_map/ppermute | solution.py:294
  58.1 19.9 %collective-permute-start.6 = (bf16[96,1152]{1,0:T(8,128)(2,1)}, bf16[96,1152]{1,0:T(8,128)(2,1)}, u32[]{:S(2)}, u32[]{:S(2)}) collective-permute-start(bf16[96,1152]{1,0:T(8,128)(2,1)} %get-tuple-element.37), channel_id=1, source_target_pairs={{0,192},{24,216},{48,240},{72,264},{96,288},{120,312},{144,336},{1... | collective-permute-start | bytes 663560 | tf_op jit(solution)/shard_map/ppermute | solution.py:295
  71.3 39.3 %all-to-all-start.1 = ((bf16[8,48,1152]{2,1,0:T(8,128)(2,1)}), bf16[8,48,1152]{2,1,0:T(8,128)(2,1)}, u32[]{:S(2)}, u32[]{:S(2)}) async-start(bf16[8,48,1152]{2,1,0:T(8,128)(2,1)} %bitcast.6), calls=%async_computation.1 | async-start | bytes 1769472 | tf_op jit(solution)/shard_map/all_to_all | solution.py:269
  79.4 10.4 %collective-permute-start.7 = (bf16[96,1280]{1,0:T(8,128)(2,1)S(1)}, bf16[96,1280]{1,0:T(8,128)(2,1)S(1)}, u32[]{:S(2)}, u32[]{:S(2)}) collective-permute-start(bf16[96,1280]{1,0:T(8,128)(2,1)S(1)} %get-tuple-element.39), channel_id=1, source_target_pairs={{0,48},{24,72},{48,0},{72,24},{96,144},{120,168},{144,96},{168,120... | collective-permute-start | bytes 737288 | tf_op jit(solution)/shard_map/ppermute | solution.py:312
  82.8 7.0 %collective-permute-start.8 = (bf16[48,1152]{1,0:T(8,128)(2,1)S(1)}, bf16[48,1152]{1,0:T(8,128)(2,1)S(1)}, u32[]{:S(2)}, u32[]{:S(2)}) collective-permute-start(bf16[48,1152]{1,0:T(8,128)(2,1)S(1)} %get-tuple-element.41), channel_id=1, source_target_pairs={{0,384},{24,408},{48,432},{72,456},{96,480},{120,504},{144,528},{1... | collective-permute-start | bytes 331784 | tf_op jit(solution)/shard_map/ppermute | solution.py:313
  90.6 11.3 %collective-permute-start.9 = (bf16[48,1280]{1,0:T(8,128)(2,1)S(1)}, bf16[48,1280]{1,0:T(8,128)(2,1)S(1)}, u32[]{:S(2)}, u32[]{:S(2)}) collective-permute-start(bf16[48,1280]{1,0:T(8,128)(2,1)S(1)} %get-tuple-element.43), channel_id=1, source_target_pairs={{0,144},{24,168},{48,96},{72,120},{96,48},{120,72},{144,0},{168,24... | collective-permute-start | bytes 368648 | tf_op jit(solution)/shard_map/ppermute | solution.py:318
  92.7 14.7 %collective-permute-start.12 = (bf16[48,1280]{1,0:T(8,128)(2,1)S(1)}, bf16[48,1280]{1,0:T(8,128)(2,1)S(1)}, u32[]{:S(2)}, u32[]{:S(2)}) collective-permute-start(bf16[48,1280]{1,0:T(8,128)(2,1)S(1)} %get-tuple-element.48), channel_id=1, source_target_pairs={{0,16},{1,17},{2,18},{3,19},{4,20},{5,21},{6,22},{7,23},{8,0},{9,1... | collective-permute-start | bytes 368648 | tf_op jit(solution)/shard_map/ppermute | solution.py:304
  96.7 13.2 %collective-permute-start.13 = (bf16[48,1280]{1,0:T(8,128)(2,1)S(1)}, bf16[48,1280]{1,0:T(8,128)(2,1)S(1)}, u32[]{:S(2)}, u32[]{:S(2)}) collective-permute-start(bf16[48,1280]{1,0:T(8,128)(2,1)S(1)} %get-tuple-element.49), channel_id=1, source_target_pairs={{0,8},{1,9},{2,10},{3,11},{4,12},{5,13},{6,14},{7,15},{8,16},{9,17... | collective-permute-start | bytes 368648 | tf_op jit(solution)/shard_map/ppermute | solution.py:305

commit v3 on v2

--- a/solution.py
+++ b/solution.py
@@ -9,7 +9,7 @@
 N_ZH, N_Y = 3, 8
 LANES = 128
 LATE = 200_000_000_000
-PREP, JOIN, STACK, CAPS, FOLD, FOLD2 = 0, LATE, 5_000_000_000, LATE, LATE, 0
+JOIN, STACK, CAPS, FOLD, FOLD2 = LATE, 5_000_000_000, LATE, LATE, 0
 
 F32, BF16 = jnp.float32, jnp.bfloat16
 SMEM = pl.BlockSpec(memory_space=pltpu.SMEM)
@@ -84,28 +84,17 @@
     return jnp.where(lane == 0, jnp.sum(extra, axis=1, keepdims=True), 0.0)
 
 
-def prepare(zh_ref, caption, image, owner, valid, count, outgoing, tag1, tag2, own_marks,
-            image_v, owner_v, valid_v, count_v, sems, more_sems):
+def tags(zh_ref, image, lists, tag1, tag2, own_marks):
     zh = zh_ref[0]
     rows, width = image.shape
-    third = owner.shape[1] // N_ZH
-    small = [
-        pltpu.make_async_copy(src, dst, more_sems.at[n])
-        for n, (src, dst) in enumerate(((owner, owner_v), (valid, valid_v), (count, count_v), (image, image_v)))
-    ]
-    copies = [
-        pltpu.make_async_copy(caption.at[lax.rem(zh + (N_ZH - k), N_ZH)], outgoing.at[:, k], sems.at[k])
-        for k in range(N_ZH)
-    ]
-    for copy in small + copies:
-        copy.start()
-    for copy in small:
-        copy.wait()
+    slots = (lists.shape[1] - rows) // 2
+    third = slots // N_ZH
+    owner, valid, count = lists[:, :slots], lists[:, slots:2 * slots], lists[:, 2 * slots:]
     diagonal = lax.broadcasted_iota(jnp.int32, (rows, rows), 0) == lax.broadcasted_iota(jnp.int32, (rows, rows), 1)
-    number = jnp.sum(jnp.where(diagonal, count_v[...].astype(F32), 0.0), axis=1, keepdims=True)
+    number = jnp.sum(jnp.where(diagonal, count.astype(F32), 0.0), axis=1, keepdims=True)
     number = jnp.maximum(number, 1.0)
-    holds = owner_v[...] == lax.broadcasted_iota(jnp.int32, (rows, N_ZH * third), 0)
-    marks = jnp.where(holds & (valid_v[...] > 0), number, 0.0).astype(BF16)
+    holds = owner == lax.broadcasted_iota(jnp.int32, (rows, slots), 0)
+    marks = jnp.where(holds & (valid > 0), number, 0.0).astype(BF16)
     parts = [marks[:, h * third:(h + 1) * third] for h in range(N_ZH)]
     for k, ref in enumerate((own_marks, tag1, tag2)):
         to = lax.rem(zh + k, N_ZH)
@@ -113,13 +102,11 @@
         if k == 0:
             ref[...] = part
         else:
-            ref[:, :width] = image_v[...]
+            ref[:, :width] = image[...]
             ref[:, width:] = part
-    for copy in copies:
-        copy.wait()
-
-
-def join(image, got_image, text, got_text, after, images, texts):
+
+
+def join(image, got_image, text, got_text, images, texts):
     for first, second, out in ((image, got_image, images), (text, got_text, texts)):
         rows = first.shape[0]
         out[:rows, :] = first[...]
@@ -176,37 +163,34 @@
     text_grad[...] = scale_ref[0] * (own_text[...] + got_text[...].astype(F32))
 
 
-def fold_both(own, got, own_text, got_text, keep, send, keep_text, send_text):
+def fold_both(own, got, own_text, got_text, cap1, keep, send, keep_text, send_text):
     fold_tagged(own, got, keep, send)
+    rows, width = cap1.shape[0], cap1.shape[1] - LANES
+    keep[:rows, :width] += cap1[:, :width].astype(F32)
+    keep[:rows, width:] += join_lanes(cap1[:, width:].astype(F32))
     half = keep_text.shape[0]
     keep_text[...] = own_text[:half, :] + got_text[:half, :].astype(F32)
     send_text[...] = (own_text[half:, :] + got_text[half:, :].astype(F32)).astype(BF16)
 
 
-def captions(scale_ref, bias_ref, arrived, image, own_marks, tag1, tag2, back, own, send1, send2,
-             here, done, in_sems, out_sems):
-    width = image.shape[1]
-    slots = arrived.shape[0] * arrived.shape[2]
+def captions(zh_ref, scale_ref, bias_ref, arrived, image, own_marks, tag1, tag2, back, own, send1, send2):
+    n_y, _, run, width = arrived.shape
+    slots = n_y * run
     scale, bias = scale_ref[0], bias_ref[0]
-    loads = [pltpu.make_async_copy(arrived.at[:, k], here.at[k], in_sems.at[k]) for k in range(N_ZH)]
-    stores = [pltpu.make_async_copy(done.at[k], back.at[:, k], out_sems.at[k]) for k in range(N_ZH)]
-    for load in loads:
-        load.start()
     for k in range(N_ZH):
+        plane = lax.rem(zh_ref[0] + (N_ZH - k), N_ZH)
         if k == 0:
             i, mark = image[...], own_marks[...].astype(F32)
         else:
             ref = (tag1, tag2)[k - 1]
             i, mark = ref[:, :width], ref[:, width:].astype(F32)
-        loads[k].wait()
-        e = here[k].reshape(slots, width)
+        e = arrived[:, plane].reshape(slots, width)
         there = mark > 0
         denom = jnp.where(there, mark, 1.0)
         loss, slope = soft_terms(-(scale * nt(i, e) + bias))
         loss = jnp.sum(jnp.where(there, loss / denom, 0.0), axis=1, keepdims=True)
         weight = jnp.where(there, -slope / denom, 0.0).astype(BF16)
-        done[k] = (scale * tn(weight, i)).astype(BF16).reshape(done.shape[1:])
-        stores[k].start()
+        back[:, plane] = (scale * tn(weight, i)).astype(BF16).reshape(n_y, run, width)
         part = nn(weight, e)
         if k == 0:
             own[:, :width] = part
@@ -215,33 +199,15 @@
             ref = (send1, send2)[k - 1]
             ref[:, :width] = part.astype(BF16)
             ref[:, width:] = split_lanes(loss_lanes(loss))
-    for store in stores:
-        store.wait()
-
-
-def finish(scale_ref, own, got, cap_own, cap1, cap2, loss, image_grad):
+
+
+def finish(scale_ref, own, got, cap_own, cap2, after, loss, image_grad):
     rows, width = image_grad.shape
-    total = own[...] + got[...].astype(F32) + cap_own[...] + cap1[...].astype(F32) + cap2[...].astype(F32)
+    total = own[...] + got[...].astype(F32) + cap_own[...] + cap2[...].astype(F32)
     image_grad[...] = scale_ref[0] * total[:, :width]
     column = jnp.sum(total[:, width:], axis=1, keepdims=True)
     diagonal = lax.broadcasted_iota(jnp.int32, (rows, rows), 0) == lax.broadcasted_iota(jnp.int32, (rows, rows), 1)
     loss[...] = jnp.sum(jnp.where(diagonal, column, 0.0), axis=0, keepdims=True)
-
-
-def place(zh_ref, back, out, here, in_sems, out_sems):
-    zh = zh_ref[0]
-    loads = [pltpu.make_async_copy(back.at[:, k], here.at[k], in_sems.at[k]) for k in range(N_ZH)]
-    stores = [
-        pltpu.make_async_copy(here.at[k], out.at[lax.rem(zh + (N_ZH - k), N_ZH)], out_sems.at[k])
-        for k in range(N_ZH)
-    ]
-    for load in loads:
-        load.start()
-    for load, store in zip(loads, stores):
-        load.wait()
-        store.start()
-    for store in stores:
-        store.wait()
 
 
 def shards(image, text, caption, logit_scale, logit_bias, owner, valid, count):
@@ -251,17 +217,10 @@
     run = slots // (N_ZH * N_Y)
     third = slots // N_ZH
     zh = (lax.axis_index("cap") // N_Y).astype(jnp.int32).reshape(1)
-    sems = pltpu.SemaphoreType.DMA((N_ZH,))
-
-    outgoing, tag1, tag2, own_marks = call(
-        prepare,
-        [((N_Y, N_ZH, run, width), BF16), ((rows, wide), BF16), ((rows, wide), BF16), ((rows, third), BF16)],
-        (zh, caption.reshape(N_ZH, N_Y, run, width), image, owner.reshape(1, slots), valid.reshape(1, slots),
-         count.reshape(1, rows)),
-        [SMEM] + [HBM] * 5, [VMEM] * 4,
-        [pltpu.VMEM((rows, width), BF16), pltpu.VMEM((1, slots), jnp.int32), pltpu.VMEM((1, slots), jnp.int32),
-         pltpu.VMEM((1, rows), jnp.int32), sems, pltpu.SemaphoreType.DMA((4,))],
-        flops=PREP, room=8,
+    lists = jnp.concatenate([owner, valid, count]).reshape(1, 2 * slots + rows)
+    tag1, tag2, own_marks = call(
+        tags, [((rows, wide), BF16), ((rows, wide), BF16), ((rows, third), BF16)], (zh, image, lists),
+        [SMEM, VMEM, VMEM],
     )
 
     def to_y(x):
@@ -269,14 +228,13 @@
         x = lax.all_to_all(x, "cap", 0, 0, axis_index_groups=Y_GROUPS, tiled=True)
         return x.reshape(N_Y, N_ZH, run, width)
 
-    arrived = to_y(outgoing)
+    arrived = to_y(caption.reshape(N_ZH, N_Y, run, width).swapaxes(0, 1))
     from1 = lax.ppermute(tag1, "cap", shift_zh(1))
     from2 = lax.ppermute(tag2, "cap", shift_zh(2))
 
     images, texts = call(
         join, [((2 * rows, width), BF16)] * 2,
-        (image, lax.ppermute(image, "blk", X_FAR), text, lax.ppermute(text, "blk", ZL_FAR), tag1),
-        [VMEM] * 4 + [ANY], flops=JOIN,
+        (image, lax.ppermute(image, "blk", X_FAR), text, lax.ppermute(text, "blk", ZL_FAR)), [VMEM] * 4, flops=JOIN,
     )
     images, texts = call(
         stack, [((4 * rows, width), BF16)] * 2,
@@ -289,7 +247,6 @@
         lambda *refs: pairs(*refs, rows=rows),
         [((n_i // 2, wide), F32), ((n_i // 2, wide), BF16), ((n_t // 2, width), F32), ((n_t // 2, width), BF16)],
         (logit_scale, logit_bias, images, others, texts), [SMEM, SMEM] + [VMEM] * 3,
-        flops=6 * n_i * n_t * width, moved=8 * n_i * width,
     )
     got = lax.ppermute(send, "blk", OTHER_CORE)
     got_t = lax.ppermute(send_t, "blk", ZL_NEAR)
@@ -297,8 +254,7 @@
     back, cap_own, send1, send2 = call(
         captions,
         [((N_Y, N_ZH, run, width), BF16), ((rows, wide), F32), ((rows, wide), BF16), ((rows, wide), BF16)],
-        (logit_scale, logit_bias, arrived, image, own_marks, from1, from2), [SMEM, SMEM, ANY] + [VMEM] * 4,
-        [ANY] + [VMEM] * 3, [pltpu.VMEM((N_ZH, N_Y, run, width), BF16)] * 2 + [sems, sems], flops=CAPS,
+        (zh, logit_scale, logit_bias, arrived, image, own_marks, from1, from2), [SMEM] * 3 + [VMEM] * 5, flops=CAPS,
     )
     returned = to_y(back)
     cap1 = lax.ppermute(send1, "cap", shift_zh(-1))
@@ -307,7 +263,7 @@
     keep, send, keep_t, send_t = call(
         fold_both,
         [((n_i // 4, wide), F32), ((n_i // 4, wide), BF16), ((rows, width), F32), ((rows, width), BF16)],
-        (keep, got, keep_t, got_t), [VMEM] * 4, flops=FOLD,
+        (keep, got, keep_t, got_t, cap1), [VMEM] * 5, flops=FOLD,
     )
     got = lax.ppermute(send, "blk", X_NEAR)
     got_t = lax.ppermute(send_t, "blk", ZL_FAR)
@@ -316,15 +272,12 @@
         (logit_scale, keep, got, keep_t, got_t), [SMEM] + [VMEM] * 4, flops=FOLD2,
     )
     got = lax.ppermute(send, "blk", X_FAR)
+    caption_grad = returned.swapaxes(0, 1).reshape(slots, width)
     loss, image_grad = call(
         finish, [((1, rows), F32), ((rows, width), F32)],
-        (logit_scale, keep, got, cap_own, cap1, cap2), [SMEM] + [VMEM] * 5, moved=rows * wide * 20,
-    )
-    (caption_grad,) = call(
-        place, [((N_ZH, N_Y, run, width), BF16)], (zh, returned), [SMEM, ANY], [ANY],
-        [pltpu.VMEM((N_ZH, N_Y, run, width), BF16), sems, sems], moved=4 * slots * width
-    )
-    return loss.reshape(rows), image_grad, text_grad, caption_grad.reshape(slots, width)
+        (logit_scale, keep, got, cap_own, cap2, caption_grad), [SMEM] + [VMEM] * 4 + [ANY],
+    )
+    return loss.reshape(rows), image_grad, text_grad, caption_grad
 
 
 def solution(mesh):

time: 114 us -> 109 us (0.956)
  Pallas kernels: 12.5 us -> 9.29 us
  starting transfers between devices: 70.4 us -> 68.9 us
    all_to_all x2, waiting for transfers between devices: 0.01 us -> 8.63 us  [to_y(): x = lax.all_to_all(x, 'cap', 0, 0, axis_index_groups=Y_GROUPS, tiled=True)]
    ppermute x1, waiting for transfers between devices: 5.06 us -> 1.1 us  [shards(): got_t = lax.ppermute(send_t, 'blk', ZL_FAR)]
    transpose x0 -> x2, local copies, waits for them, and re-layouts: none -> 3.38 us  [the longest x1 2.15 us: shards(): arrived = to_y(caption.reshape(N_ZH, N_Y, run, width).swapaxes(0, 1))]
    unnamed x14 -> x12, local copies, waits for them, and re-layouts: 4.08 us -> 0.8 us
    pallas_call x9 -> x8, Pallas kernels: 12.5 us -> 9.29 us  [call(): pl.pallas_call(body, out_shape=tuple((jax.ShapeDtypeStruct(s, d) for s, d...]
    ppermute x1, waiting for transfers between devices: 5.47 us -> 2.6 us  [shards(): cap1 = lax.ppermute(send1, 'cap', shift_zh(-1))]
    ppermute x1, waiting for transfers between devices: 2.45 us -> 0.01 us  [shards(): cap2 = lax.ppermute(send2, 'cap', shift_zh(-2))]
    ppermute x1, starting transfers between devices: 5.22 us -> 3.76 us  [shards(): cap2 = lax.ppermute(send2, 'cap', shift_zh(-2))]
  transfers between devices with their start and end apart: 16 -> 16, of which waited for: 6 -> 6; matrix products, arithmetic and copies ran while one was open for 0% -> 3% of each run, Pallas kernels for 9% -> 8%
where the time goes in v3:
time: 109 us; the launch traced here: 107 us
  starting transfers between devices  68.9 us (63%)
  waiting for transfers between devices  22.5 us (21%)
  Pallas kernels  9.29 us (9%)
  local copies, waits for them, and re-layouts  4.19 us (4%)
  between operations  2.22 us (2%)
    all_to_all x2, starting transfers between devices, to_y(): x = lax.all_to_all(x, 'cap', 0, 0, axis_index_groups=Y_GROUPS, tiled=True)  13.7 us
    ppermute x1, starting transfers between devices, shards(): from1 = lax.ppermute(tag1, 'cap', shift_zh(1))  10.3 us
    pallas_call x8, Pallas kernels, call(): pl.pallas_call(body, out_shape=tuple((jax.ShapeDtypeStruct(s, d) for s, d...  9.29 us
    all_to_all x2, waiting for transfers between devices, to_y(): x = lax.all_to_all(x, 'cap', 0, 0, axis_index_groups=Y_GROUPS, tiled=True)  8.63 us
    ppermute x1, starting transfers between devices, shards(): lax.ppermute(text, 'blk', ZL_FAR)  6.64 us
    ppermute x1, waiting for transfers between devices, shards(): from2 = lax.ppermute(tag2, 'cap', shift_zh(2))  6.07 us
    ppermute x1, starting transfers between devices, shards(): lax.ppermute(image, 'blk', X_FAR)  4.39 us
    ppermute x1, starting transfers between devices, shards(): others = lax.ppermute(images, 'blk', OTHER_CORE)  4.17 us
  transfers between devices with their start and end apart: 16, of which 6 were waited for; matrix products, arithmetic and copies ran while one was open for 3% of the time, Pallas kernels for 8%

profile of v3, /device:TPU:1, one launch (start us, length us, event | category | flops | bytes accessed | tf_op | source)
XLA Modules:
  0.0 107.1 jit_solution(11669860809718566720)
XLA Ops:
  0.6 6.6 %collective-permute-start.1 = (bf16[48,1152]{1,0:T(8,128)(2,1)}, bf16[48,1152]{1,0:T(8,128)(2,1)S(1)}, u32[]{:S(2)}, u32[]{:S(2)}) collective-permute-start(bf16[48,1152]{1,0:T(8,128)(2,1)} %text.1), channel_id=1, source_target_pairs={{0,384},{24,408},{48,432},{72,456},{96,480},{120,504},{144,528},{1... | collective-permute-start | bytes 331784 | tf_op jit(solution)/shard_map/ppermute | solution.py:237
  7.3 4.4 %collective-permute-start = (bf16[48,1152]{1,0:T(8,128)(2,1)}, bf16[48,1152]{1,0:T(8,128)(2,1)S(1)}, u32[]{:S(2)}, u32[]{:S(2)}) collective-permute-start(bf16[48,1152]{1,0:T(8,128)(2,1)} %image.5), channel_id=1, source_target_pairs={{0,144},{24,168},{48,96},{72,120},{96,48},{120,72},{144,0},{168,24... | collective-permute-start | bytes 331784 | tf_op jit(solution)/shard_map/ppermute | solution.py:237
  11.7 2.1 %copy.13 = bf16[8,3,16,1152]{3,2,1,0:T(8,128)(2,1)} copy(bf16[8,3,16,1152]{3,2,0,1:T(8,128)(2,1)} %bitcast.14) | data formatting | bytes 1769472 | tf_op jit(solution)/shard_map/transpose | solution.py:231
  13.8 7.0 %all-to-all-start = ((bf16[8,48,1152]{2,1,0:T(8,128)(2,1)}), bf16[8,48,1152]{2,1,0:T(8,128)(2,1)}, u32[]{:S(2)}, u32[]{:S(2)}) async-start(bf16[8,48,1152]{2,1,0:T(8,128)(2,1)} %bitcast.3), calls=%async_computation | async-start | bytes 1769472 | tf_op jit(solution)/shard_map/all_to_all | solution.py:228
  20.9 1.9 %collective-permute-start.2 = (bf16[96,1152]{1,0:T(8,128)(2,1)S(1)}, bf16[96,1152]{1,0:T(8,128)(2,1)S(1)}, u32[]{:S(2)}, u32[]{:S(2)}) collective-permute-start(bf16[96,1152]{1,0:T(8,128)(2,1)S(1)} %get-tuple-element.28.images1), channel_id=1, source_target_pairs={{0,48},{24,72},{48,0},{72,24},{96,144},{120,168},{144,96},{168,120... | collective-permute-start | bytes 663560 | tf_op jit(solution)/shard_map/ppermute | solution.py:241
  22.8 4.0 %collective-permute-start.3 = (bf16[96,1152]{1,0:T(8,128)(2,1)S(1)}, bf16[96,1152]{1,0:T(8,128)(2,1)S(1)}, u32[]{:S(2)}, u32[]{:S(2)}) collective-permute-start(bf16[96,1152]{1,0:T(8,128)(2,1)S(1)} %get-tuple-element.29.texts1), channel_id=1, source_target_pairs={{0,192},{24,216},{48,240},{72,264},{96,288},{120,312},{144,336},{1... | collective-permute-start | bytes 663560 | tf_op jit(solution)/shard_map/ppermute | solution.py:241
  26.8 1.5 %collective-permute-done.2.images2 = bf16[96,1152]{1,0:T(8,128)(2,1)S(1)} collective-permute-done((bf16[96,1152]{1,0:T(8,128)(2,1)S(1)}, bf16[96,1152]{1,0:T(8,128)(2,1)S(1)}, u32[]{:S(2)}, u32[]{:S(2)}) %collective-permute-start.2) | collective-permute-done | bytes 221216 | tf_op jit(solution)/shard_map/ppermute | solution.py:241
  28.3 2.6 %collective-permute-done.3.texts2 = bf16[96,1152]{1,0:T(8,128)(2,1)S(1)} collective-permute-done((bf16[96,1152]{1,0:T(8,128)(2,1)S(1)}, bf16[96,1152]{1,0:T(8,128)(2,1)S(1)}, u32[]{:S(2)}, u32[]{:S(2)}) %collective-permute-start.3) | collective-permute-done | bytes 221216 | tf_op jit(solution)/shard_map/ppermute | solution.py:241
  31.0 4.2 %collective-permute-start.4 = (bf16[192,1152]{1,0:T(8,128)(2,1)S(1)}, bf16[192,1152]{1,0:T(8,128)(2,1)S(1)}, u32[]{:S(2)}, u32[]{:S(2)}) collective-permute-start(bf16[192,1152]{1,0:T(8,128)(2,1)S(1)} %get-tuple-element.30.refs_2_), channel_id=1, source_target_pairs={{0,24},{24,0},{48,72},{72,48},{96,120},{120,96},{144,168},{168,144... | collective-permute-start | bytes 1327112 | tf_op jit(solution)/shard_map/ppermute | solution.py:244
  36.0 10.3 %collective-permute-start.7 = (bf16[48,1280]{1,0:T(8,128)(2,1)S(1)}, bf16[48,1280]{1,0:T(8,128)(2,1)S(1)}, u32[]{:S(2)}, u32[]{:S(2)}) collective-permute-start(bf16[48,1280]{1,0:T(8,128)(2,1)S(1)} %get-tuple-element.37), channel_id=1, source_target_pairs={{0,8},{1,9},{2,10},{3,11},{4,12},{5,13},{6,14},{7,15},{8,16},{9,17... | collective-permute-start | bytes 368648 | tf_op jit(solution)/shard_map/ppermute | solution.py:232
  46.4 3.4 %collective-permute-start.8 = (bf16[48,1280]{1,0:T(8,128)(2,1)S(1)}, bf16[48,1280]{1,0:T(8,128)(2,1)S(1)}, u32[]{:S(2)}, u32[]{:S(2)}) collective-permute-start(bf16[48,1280]{1,0:T(8,128)(2,1)S(1)} %get-tuple-element.38), channel_id=1, source_target_pairs={{0,16},{1,17},{2,18},{3,19},{4,20},{5,21},{6,22},{7,23},{8,0},{9,1... | collective-permute-start | bytes 368648 | tf_op jit(solution)/shard_map/ppermute | solution.py:233
  51.1 2.3 %shard_map.113 = (f32[192,1280]{1,0:T(8,128)S(1)}, bf16[192,1280]{1,0:T(8,128)(2,1)}, f32[96,1152]{1,0:T(8,128)S(1)}, bf16[96,1152]{1,0:T(8,128)(2,1)}) custom-call(f32[1]{0:T(128)S(6)} %copy.15.refs_0_.scale_ref, f32[1]{0:T(128)S(6)} %copy.16.refs_1_.bias_ref, bf16[192,1152]{1,0:T(8,128)(2,1)S(1)} %get-tuple-element.30.refs_2_, ...), custom_call_target="tpu_custom_call" | custom-call | tf_op jit(solution)/shard_map/pallas_call | solution.py:42
  53.4 3.1 %collective-permute-start.6 = (bf16[96,1152]{1,0:T(8,128)(2,1)}, bf16[96,1152]{1,0:T(8,128)(2,1)}, u32[]{:S(2)}, u32[]{:S(2)}) collective-permute-start(bf16[96,1152]{1,0:T(8,128)(2,1)} %get-tuple-element.35), channel_id=1, source_target_pairs={{0,192},{24,216},{48,240},{72,264},{96,288},{120,312},{144,336},{1... | collective-permute-start | bytes 663560 | tf_op jit(solution)/shard_map/ppermute | solution.py:252
  56.5 2.5 %collective-permute-start.5 = (bf16[192,1280]{1,0:T(8,128)(2,1)}, bf16[192,1280]{1,0:T(8,128)(2,1)}, u32[]{:S(2)}, u32[]{:S(2)}) collective-permute-start(bf16[192,1280]{1,0:T(8,128)(2,1)} %get-tuple-element.33), channel_id=1, source_target_pairs={{0,24},{24,0},{48,72},{72,48},{96,120},{120,96},{144,168},{168,144... | collective-permute-start | bytes 1474568 | tf_op jit(solution)/shard_map/ppermute | solution.py:251
  59.0 6.1 %collective-permute-done.8.tag2 = bf16[48,1280]{1,0:T(8,128)(2,1)S(1)} collective-permute-done((bf16[48,1280]{1,0:T(8,128)(2,1)S(1)}, bf16[48,1280]{1,0:T(8,128)(2,1)S(1)}, u32[]{:S(2)}, u32[]{:S(2)}) %collective-permute-start.8) | collective-permute-done | bytes 122912 | tf_op jit(solution)/shard_map/ppermute | solution.py:233
  65.1 3.6 %shard_map.115 = (bf16[8,3,16,1152]{3,2,1,0:T(8,128)(2,1)}, f32[48,1280]{1,0:T(8,128)S(1)}, bf16[48,1280]{1,0:T(8,128)(2,1)S(1)}, bf16[48,1280]{1,0:T(8,128)(2,1)S(1)}) custom-call(s32[1]{0:T(128)} %bitcast.zh_ref, f32[1]{0:T(128)S(6)} %copy.15.refs_0_.scale_ref, f32[1]{0:T(128)S(6)} %copy.16.refs_1_.bias_ref, bf16[8,3,16,1152]{3,2,1,0:T(8,128)(2,1)} %bitcast.4.arrived, ...), custom_call_target="tpu_custom_call" | custom-call | flops 199999995904 | tf_op jit(solution)/shard_map/pallas_call | solution.py:42
  68.7 3.6 %collective-permute-start.9 = (bf16[48,1280]{1,0:T(8,128)(2,1)S(1)}, bf16[48,1280]{1,0:T(8,128)(2,1)S(1)}, u32[]{:S(2)}, u32[]{:S(2)}) collective-permute-start(bf16[48,1280]{1,0:T(8,128)(2,1)S(1)} %get-tuple-element.39), channel_id=1, source_target_pairs={{0,16},{1,17},{2,18},{3,19},{4,20},{5,21},{6,22},{7,23},{8,0},{9,1... | collective-permute-start | bytes 368648 | tf_op jit(solution)/shard_map/ppermute | solution.py:260
  72.4 6.7 %all-to-all-start.1 = ((bf16[8,48,1152]{2,1,0:T(8,128)(2,1)}), bf16[8,48,1152]{2,1,0:T(8,128)(2,1)}, u32[]{:S(2)}, u32[]{:S(2)}) async-start(bf16[8,48,1152]{2,1,0:T(8,128)(2,1)} %bitcast.5), calls=%async_computation.1 | async-start | bytes 1769472 | tf_op jit(solution)/shard_map/all_to_all | solution.py:228
  79.1 2.6 %collective-permute-done.9.cap1 = bf16[48,1280]{1,0:T(8,128)(2,1)S(1)} collective-permute-done((bf16[48,1280]{1,0:T(8,128)(2,1)S(1)}, bf16[48,1280]{1,0:T(8,128)(2,1)S(1)}, u32[]{:S(2)}, u32[]{:S(2)}) %collective-permute-start.9) | collective-permute-done | bytes 122912 | tf_op jit(solution)/shard_map/ppermute | solution.py:260
  83.2 3.4 %collective-permute-start.10 = (bf16[96,1280]{1,0:T(8,128)(2,1)S(1)}, bf16[96,1280]{1,0:T(8,128)(2,1)S(1)}, u32[]{:S(2)}, u32[]{:S(2)}) collective-permute-start(bf16[96,1280]{1,0:T(8,128)(2,1)S(1)} %get-tuple-element.41), channel_id=1, source_target_pairs={{0,48},{24,72},{48,0},{72,24},{96,144},{120,168},{144,96},{168,120... | collective-permute-start | bytes 737288 | tf_op jit(solution)/shard_map/ppermute | solution.py:268
  86.5 1.9 %collective-permute-start.11 = (bf16[48,1152]{1,0:T(8,128)(2,1)S(1)}, bf16[48,1152]{1,0:T(8,128)(2,1)S(1)}, u32[]{:S(2)}, u32[]{:S(2)}) collective-permute-start(bf16[48,1152]{1,0:T(8,128)(2,1)S(1)} %get-tuple-element.43), channel_id=1, source_target_pairs={{0,384},{24,408},{48,432},{72,456},{96,480},{120,504},{144,528},{1... | collective-permute-start | bytes 331784 | tf_op jit(solution)/shard_map/ppermute | solution.py:269
  88.5 3.8 %collective-permute-start.13 = (bf16[48,1280]{1,0:T(8,128)(2,1)S(1)}, bf16[48,1280]{1,0:T(8,128)(2,1)S(1)}, u32[]{:S(2)}, u32[]{:S(2)}) collective-permute-start(bf16[48,1280]{1,0:T(8,128)(2,1)S(1)} %get-tuple-element.47), channel_id=1, source_target_pairs={{0,8},{1,9},{2,10},{3,11},{4,12},{5,13},{6,14},{7,15},{8,16},{9,17... | collective-permute-start | bytes 368648 | tf_op jit(solution)/shard_map/ppermute | solution.py:261
  94.2 2.1 %collective-permute-start.12 = (bf16[48,1280]{1,0:T(8,128)(2,1)S(1)}, bf16[48,1280]{1,0:T(8,128)(2,1)S(1)}, u32[]{:S(2)}, u32[]{:S(2)}) collective-permute-start(bf16[48,1280]{1,0:T(8,128)(2,1)S(1)} %get-tuple-element.45), channel_id=1, source_target_pairs={{0,144},{24,168},{48,96},{72,120},{96,48},{120,72},{144,0},{168,24... | collective-permute-start | bytes 368648 | tf_op jit(solution)/shard_map/ppermute | solution.py:274
  96.3 8.6 %all-to-all-done.1 = bf16[8,48,1152]{2,1,0:T(8,128)(2,1)} async-done(((bf16[8,48,1152]{2,1,0:T(8,128)(2,1)}), bf16[8,48,1152]{2,1,0:T(8,128)(2,1)}, u32[]{:S(2)}, u32[]{:S(2)}) %all-to-all-start.1) | async-done | bytes 884768 | tf_op jit(solution)/shard_map/all_to_all | solution.py:228
  (32 shorter events, 6.5 us)
Async XLA Ops:
  0.6 20.2 %collective-permute-start.1 = (bf16[48,1152]{1,0:T(8,128)(2,1)}, bf16[48,1152]{1,0:T(8,128)(2,1)S(1)}, u32[]{:S(2)}, u32[]{:S(2)}) collective-permute-start(bf16[48,1152]{1,0:T(8,128)(2,1)} %text.1), channel_id=1, source_target_pairs={{0,384},{24,408},{48,432},{72,456},{96,480},{120,504},{144,528},{1... | collective-permute-start | bytes 331784 | tf_op jit(solution)/shard_map/ppermute | solution.py:237
  7.3 13.5 %collective-permute-start = (bf16[48,1152]{1,0:T(8,128)(2,1)}, bf16[48,1152]{1,0:T(8,128)(2,1)S(1)}, u32[]{:S(2)}, u32[]{:S(2)}) collective-permute-start(bf16[48,1152]{1,0:T(8,128)(2,1)} %image.5), channel_id=1, source_target_pairs={{0,144},{24,168},{48,96},{72,120},{96,48},{120,72},{144,0},{168,24... | collective-permute-start | bytes 331784 | tf_op jit(solution)/shard_map/ppermute | solution.py:237
  13.8 7.0 %copy-start.1 = (bf16[48,1152]{1,0:T(8,128)(2,1)S(1)}, bf16[48,1152]{1,0:T(8,128)(2,1)}, u32[]{:S(2)}) copy-start(bf16[48,1152]{1,0:T(8,128)(2,1)} %image.5) | copy-start | bytes 331780
  13.8 7.0 %copy-start.2 = (bf16[48,1152]{1,0:T(8,128)(2,1)S(1)}, bf16[48,1152]{1,0:T(8,128)(2,1)}, u32[]{:S(2)}) copy-start(bf16[48,1152]{1,0:T(8,128)(2,1)} %text.1) | copy-start | bytes 331780
  13.8 51.3 %all-to-all-start = ((bf16[8,48,1152]{2,1,0:T(8,128)(2,1)}), bf16[8,48,1152]{2,1,0:T(8,128)(2,1)}, u32[]{:S(2)}, u32[]{:S(2)}) async-start(bf16[8,48,1152]{2,1,0:T(8,128)(2,1)} %bitcast.3), calls=%async_computation | async-start | bytes 1769472 | tf_op jit(solution)/shard_map/all_to_all | solution.py:228
  20.9 7.4 %collective-permute-start.2 = (bf16[96,1152]{1,0:T(8,128)(2,1)S(1)}, bf16[96,1152]{1,0:T(8,128)(2,1)S(1)}, u32[]{:S(2)}, u32[]{:S(2)}) collective-permute-start(bf16[96,1152]{1,0:T(8,128)(2,1)S(1)} %get-tuple-element.28.images1), channel_id=1, source_target_pairs={{0,48},{24,72},{48,0},{72,24},{96,144},{120,168},{144,96},{168,120... | collective-permute-start | bytes 663560 | tf_op jit(solution)/shard_map/ppermute | solution.py:241
  22.8 8.1 %collective-permute-start.3 = (bf16[96,1152]{1,0:T(8,128)(2,1)S(1)}, bf16[96,1152]{1,0:T(8,128)(2,1)S(1)}, u32[]{:S(2)}, u32[]{:S(2)}) collective-permute-start(bf16[96,1152]{1,0:T(8,128)(2,1)S(1)} %get-tuple-element.29.texts1), channel_id=1, source_target_pairs={{0,192},{24,216},{48,240},{72,264},{96,288},{120,312},{144,336},{1... | collective-permute-start | bytes 663560 | tf_op jit(solution)/shard_map/ppermute | solution.py:241
  31.0 20.1 %collective-permute-start.4 = (bf16[192,1152]{1,0:T(8,128)(2,1)S(1)}, bf16[192,1152]{1,0:T(8,128)(2,1)S(1)}, u32[]{:S(2)}, u32[]{:S(2)}) collective-permute-start(bf16[192,1152]{1,0:T(8,128)(2,1)S(1)} %get-tuple-element.30.refs_2_), channel_id=1, source_target_pairs={{0,24},{24,0},{48,72},{72,48},{96,120},{120,96},{144,168},{168,144... | collective-permute-start | bytes 1327112 | tf_op jit(solution)/shard_map/ppermute | solution.py:244
  35.2 0.7 copy-start.4
  35.2 0.7 copy-start.3
  35.2 0.7 copy-start.5
  36.0 23.0 %collective-permute-start.7 = (bf16[48,1280]{1,0:T(8,128)(2,1)S(1)}, bf16[48,1280]{1,0:T(8,128)(2,1)S(1)}, u32[]{:S(2)}, u32[]{:S(2)}) collective-permute-start(bf16[48,1280]{1,0:T(8,128)(2,1)S(1)} %get-tuple-element.37), channel_id=1, source_target_pairs={{0,8},{1,9},{2,10},{3,11},{4,12},{5,13},{6,14},{7,15},{8,16},{9,17... | collective-permute-start | bytes 368648 | tf_op jit(solution)/shard_map/ppermute | solution.py:232
  46.4 18.7 %collective-permute-start.8 = (bf16[48,1280]{1,0:T(8,128)(2,1)S(1)}, bf16[48,1280]{1,0:T(8,128)(2,1)S(1)}, u32[]{:S(2)}, u32[]{:S(2)}) collective-permute-start(bf16[48,1280]{1,0:T(8,128)(2,1)S(1)} %get-tuple-element.38), channel_id=1, source_target_pairs={{0,16},{1,17},{2,18},{3,19},{4,20},{5,21},{6,22},{7,23},{8,0},{9,1... | collective-permute-start | bytes 368648 | tf_op jit(solution)/shard_map/ppermute | solution.py:233
  53.4 25.7 %collective-permute-start.6 = (bf16[96,1152]{1,0:T(8,128)(2,1)}, bf16[96,1152]{1,0:T(8,128)(2,1)}, u32[]{:S(2)}, u32[]{:S(2)}) collective-permute-start(bf16[96,1152]{1,0:T(8,128)(2,1)} %get-tuple-element.35), channel_id=1, source_target_pairs={{0,192},{24,216},{48,240},{72,264},{96,288},{120,312},{144,336},{1... | collective-permute-start | bytes 663560 | tf_op jit(solution)/shard_map/ppermute | solution.py:252
  56.5 22.6 %collective-permute-start.5 = (bf16[192,1280]{1,0:T(8,128)(2,1)}, bf16[192,1280]{1,0:T(8,128)(2,1)}, u32[]{:S(2)}, u32[]{:S(2)}) collective-permute-start(bf16[192,1280]{1,0:T(8,128)(2,1)} %get-tuple-element.33), channel_id=1, source_target_pairs={{0,24},{24,0},{48,72},{72,48},{96,120},{120,96},{144,168},{168,144... | collective-permute-start | bytes 1474568 | tf_op jit(solution)/shard_map/ppermute | solution.py:251
  68.7 13.0 %collective-permute-start.9 = (bf16[48,1280]{1,0:T(8,128)(2,1)S(1)}, bf16[48,1280]{1,0:T(8,128)(2,1)S(1)}, u32[]{:S(2)}, u32[]{:S(2)}) collective-permute-start(bf16[48,1280]{1,0:T(8,128)(2,1)S(1)} %get-tuple-element.39), channel_id=1, source_target_pairs={{0,16},{1,17},{2,18},{3,19},{4,20},{5,21},{6,22},{7,23},{8,0},{9,1... | collective-permute-start | bytes 368648 | tf_op jit(solution)/shard_map/ppermute | solution.py:260
  72.4 32.5 %all-to-all-start.1 = ((bf16[8,48,1152]{2,1,0:T(8,128)(2,1)}), bf16[8,48,1152]{2,1,0:T(8,128)(2,1)}, u32[]{:S(2)}, u32[]{:S(2)}) async-start(bf16[8,48,1152]{2,1,0:T(8,128)(2,1)} %bitcast.5), calls=%async_computation.1 | async-start | bytes 1769472 | tf_op jit(solution)/shard_map/all_to_all | solution.py:228
  83.2 10.2 %collective-permute-start.10 = (bf16[96,1280]{1,0:T(8,128)(2,1)S(1)}, bf16[96,1280]{1,0:T(8,128)(2,1)S(1)}, u32[]{:S(2)}, u32[]{:S(2)}) collective-permute-start(bf16[96,1280]{1,0:T(8,128)(2,1)S(1)} %get-tuple-element.41), channel_id=1, source_target_pairs={{0,48},{24,72},{48,0},{72,24},{96,144},{120,168},{144,96},{168,120... | collective-permute-start | bytes 737288 | tf_op jit(solution)/shard_map/ppermute | solution.py:268
  86.5 6.8 %collective-permute-start.11 = (bf16[48,1152]{1,0:T(8,128)(2,1)S(1)}, bf16[48,1152]{1,0:T(8,128)(2,1)S(1)}, u32[]{:S(2)}, u32[]{:S(2)}) collective-permute-start(bf16[48,1152]{1,0:T(8,128)(2,1)S(1)} %get-tuple-element.43), channel_id=1, source_target_pairs={{0,384},{24,408},{48,432},{72,456},{96,480},{120,504},{144,528},{1... | collective-permute-start | bytes 331784 | tf_op jit(solution)/shard_map/ppermute | solution.py:269
  88.5 17.7 %collective-permute-start.13 = (bf16[48,1280]{1,0:T(8,128)(2,1)S(1)}, bf16[48,1280]{1,0:T(8,128)(2,1)S(1)}, u32[]{:S(2)}, u32[]{:S(2)}) collective-permute-start(bf16[48,1280]{1,0:T(8,128)(2,1)S(1)} %get-tuple-element.47), channel_id=1, source_target_pairs={{0,8},{1,9},{2,10},{3,11},{4,12},{5,13},{6,14},{7,15},{8,16},{9,17... | collective-permute-start | bytes 368648 | tf_op jit(solution)/shard_map/ppermute | solution.py:261
  94.2 12.0 %collective-permute-start.12 = (bf16[48,1280]{1,0:T(8,128)(2,1)S(1)}, bf16[48,1280]{1,0:T(8,128)(2,1)S(1)}, u32[]{:S(2)}, u32[]{:S(2)}) collective-permute-start(bf16[48,1280]{1,0:T(8,128)(2,1)S(1)} %get-tuple-element.45), channel_id=1, source_target_pairs={{0,144},{24,168},{48,96},{72,120},{96,48},{120,72},{144,0},{168,24... | collective-permute-start | bytes 368648 | tf_op jit(solution)/shard_map/ppermute | solution.py:274
  106.2 1.0 copy-start

commit v4 on v3

--- a/solution.py
+++ b/solution.py
@@ -35,7 +35,11 @@
 
 
 def shift_zh(k):
-    return [(h * N_Y + y, ((h + k) % N_ZH) * N_Y + y) for h in range(N_ZH) for y in range(N_Y)]
+    groups = N_ZH * N_Y
+    return [
+        (b * groups + h * N_Y + y, b * groups + (h + (1 - 2 * (b % N_C)) * k) % N_ZH * N_Y + y)
+        for b in range(N_ZL * N_X * N_C) for h in range(N_ZH) for y in range(N_Y)
+    ]
 
 
 def call(body, outs, ins, in_specs, out_specs=None, scratch=(), flops=0, moved=0, room=8):
@@ -85,7 +89,7 @@
 
 
 def tags(zh_ref, image, lists, tag1, tag2, own_marks):
-    zh = zh_ref[0]
+    zh, way = zh_ref[0], zh_ref[1]
     rows, width = image.shape
     slots = (lists.shape[1] - rows) // 2
     third = slots // N_ZH
@@ -97,7 +101,7 @@
     marks = jnp.where(holds & (valid > 0), number, 0.0).astype(BF16)
     parts = [marks[:, h * third:(h + 1) * third] for h in range(N_ZH)]
     for k, ref in enumerate((own_marks, tag1, tag2)):
-        to = lax.rem(zh + k, N_ZH)
+        to = lax.rem(zh + N_ZH + way * k, N_ZH)
         part = jnp.where(to == 0, parts[0], jnp.where(to == 1, parts[1], parts[2]))
         if k == 0:
             ref[...] = part
@@ -178,7 +182,7 @@
     slots = n_y * run
     scale, bias = scale_ref[0], bias_ref[0]
     for k in range(N_ZH):
-        plane = lax.rem(zh_ref[0] + (N_ZH - k), N_ZH)
+        plane = lax.rem(zh_ref[0] + N_ZH - zh_ref[1] * k, N_ZH)
         if k == 0:
             i, mark = image[...], own_marks[...].astype(F32)
         else:
@@ -216,7 +220,7 @@
     slots = caption.shape[0]
     run = slots // (N_ZH * N_Y)
     third = slots // N_ZH
-    zh = (lax.axis_index("cap") // N_Y).astype(jnp.int32).reshape(1)
+    zh = jnp.stack([lax.axis_index("cap") // N_Y, 1 - 2 * lax.rem(lax.axis_index("blk"), N_C)]).astype(jnp.int32)
     lists = jnp.concatenate([owner, valid, count]).reshape(1, 2 * slots + rows)
     tag1, tag2, own_marks = call(
         tags, [((rows, wide), BF16), ((rows, wide), BF16), ((rows, third), BF16)], (zh, image, lists),
@@ -229,8 +233,8 @@
         return x.reshape(N_Y, N_ZH, run, width)
 
     arrived = to_y(caption.reshape(N_ZH, N_Y, run, width).swapaxes(0, 1))
-    from1 = lax.ppermute(tag1, "cap", shift_zh(1))
-    from2 = lax.ppermute(tag2, "cap", shift_zh(2))
+    from1 = lax.ppermute(tag1, ("blk", "cap"), shift_zh(1))
+    from2 = lax.ppermute(tag2, ("blk", "cap"), shift_zh(2))
 
     images, texts = call(
         join, [((2 * rows, width), BF16)] * 2,
@@ -257,8 +261,8 @@
         (zh, logit_scale, logit_bias, arrived, image, own_marks, from1, from2), [SMEM] * 3 + [VMEM] * 5, flops=CAPS,
     )
     returned = to_y(back)
-    cap1 = lax.ppermute(send1, "cap", shift_zh(-1))
-    cap2 = lax.ppermute(send2, "cap", shift_zh(-2))
+    cap1 = lax.ppermute(send1, ("blk", "cap"), shift_zh(-1))
+    cap2 = lax.ppermute(send2, ("blk", "cap"), shift_zh(-2))
 
     keep, send, keep_t, send_t = call(
         fold_both,

time: 109 us -> 105 us (0.963); the launches traced: 107 us -> 104 us
  waiting for transfers between devices: 22.5 us -> 12.2 us
  starting transfers between devices: 68.9 us -> 75.8 us
    ppermute x4, waiting for transfers between devices: 8.68 us -> 0.01 us  [the longest x1 0.01 us: shards(): from1 = lax.ppermute(tag1, ('blk', 'cap'), shift_zh(1))]
    ppermute x4, starting transfers between devices: 21.2 us -> 25.6 us  [the longest x1 11.8 us: shards(): from1 = lax.ppermute(tag1, ('blk', 'cap'), shift_zh(1))]
    ppermute x1, starting transfers between devices: 1.92 us -> 4.28 us  [shards(): got_t = lax.ppermute(send_t, 'blk', ZL_FAR)]
    ppermute x1, waiting for transfers between devices: 1.1 us -> 0.01 us  [shards(): got_t = lax.ppermute(send_t, 'blk', ZL_FAR)]
  transfers between devices with their start and end apart: 16 -> 16, of which waited for: 6 -> 3; matrix products, arithmetic and copies ran while one was open for 3% -> 3% of each run, Pallas kernels for 8% -> 9%
where the time goes in v4:
time: 105 us; the launch traced here: 104 us
  starting transfers between devices  75.8 us (72%)
  waiting for transfers between devices  12.2 us (12%)
  Pallas kernels  9.86 us (9%)
  local copies, waits for them, and re-layouts  4.19 us (4%)
  between operations  2.26 us (2%)
    all_to_all x2, starting transfers between devices, to_y(): x = lax.all_to_all(x, 'cap', 0, 0, axis_index_groups=Y_GROUPS, tiled=True)  13.7 us
    ppermute x1, starting transfers between devices, shards(): from1 = lax.ppermute(tag1, ('blk', 'cap'), shift_zh(1))  11.8 us
    pallas_call x8, Pallas kernels, call(): pl.pallas_call(body, out_shape=tuple((jax.ShapeDtypeStruct(s, d) for s, d...  9.86 us
    all_to_all x2, waiting for transfers between devices, to_y(): x = lax.all_to_all(x, 'cap', 0, 0, axis_index_groups=Y_GROUPS, tiled=True)  8.11 us
    ppermute x1, starting transfers between devices, shards(): lax.ppermute(text, 'blk', ZL_FAR)  6.64 us
    ppermute x1, starting transfers between devices, shards(): cap1 = lax.ppermute(send1, ('blk', 'cap'), shift_zh(-1))  6.3 us
    ppermute x1, starting transfers between devices, shards(): cap2 = lax.ppermute(send2, ('blk', 'cap'), shift_zh(-2))  5.5 us
    ppermute x1, starting transfers between devices, shards(): lax.ppermute(image, 'blk', X_FAR)  4.39 us
  transfers between devices with their start and end apart: 16, of which 3 were waited for; matrix products, arithmetic and copies ran while one was open for 3% of the time, Pallas kernels for 9%

profile of v4, /device:TPU:1, one launch (start us, length us, event | category | flops | bytes accessed | tf_op | source)
XLA Modules:
  0.0 104.4 jit_solution(13074118761618938415)
XLA Ops:
  0.6 6.6 %collective-permute-start.1 = (bf16[48,1152]{1,0:T(8,128)(2,1)}, bf16[48,1152]{1,0:T(8,128)(2,1)S(1)}, u32[]{:S(2)}, u32[]{:S(2)}) collective-permute-start(bf16[48,1152]{1,0:T(8,128)(2,1)} %text.1), channel_id=1, source_target_pairs={{0,384},{24,408},{48,432},{72,456},{96,480},{120,504},{144,528},{1... | collective-permute-start | bytes 331784 | tf_op jit(solution)/shard_map/ppermute | solution.py:241
  7.3 4.4 %collective-permute-start = (bf16[48,1152]{1,0:T(8,128)(2,1)}, bf16[48,1152]{1,0:T(8,128)(2,1)S(1)}, u32[]{:S(2)}, u32[]{:S(2)}) collective-permute-start(bf16[48,1152]{1,0:T(8,128)(2,1)} %image.5), channel_id=1, source_target_pairs={{0,144},{24,168},{48,96},{72,120},{96,48},{120,72},{144,0},{168,24... | collective-permute-start | bytes 331784 | tf_op jit(solution)/shard_map/ppermute | solution.py:241
  11.7 2.1 %copy.13 = bf16[8,3,16,1152]{3,2,1,0:T(8,128)(2,1)} copy(bf16[8,3,16,1152]{3,2,0,1:T(8,128)(2,1)} %bitcast.15) | data formatting | bytes 1769472 | tf_op jit(solution)/shard_map/transpose | solution.py:235
  13.8 7.0 %all-to-all-start = ((bf16[8,48,1152]{2,1,0:T(8,128)(2,1)}), bf16[8,48,1152]{2,1,0:T(8,128)(2,1)}, u32[]{:S(2)}, u32[]{:S(2)}) async-start(bf16[8,48,1152]{2,1,0:T(8,128)(2,1)} %bitcast.4), calls=%async_computation | async-start | bytes 1769472 | tf_op jit(solution)/shard_map/all_to_all | solution.py:232
  20.9 1.9 %collective-permute-start.2 = (bf16[96,1152]{1,0:T(8,128)(2,1)S(1)}, bf16[96,1152]{1,0:T(8,128)(2,1)S(1)}, u32[]{:S(2)}, u32[]{:S(2)}) collective-permute-start(bf16[96,1152]{1,0:T(8,128)(2,1)S(1)} %get-tuple-element.28.images1), channel_id=1, source_target_pairs={{0,48},{24,72},{48,0},{72,24},{96,144},{120,168},{144,96},{168,120... | collective-permute-start | bytes 663560 | tf_op jit(solution)/shard_map/ppermute | solution.py:245
  22.8 4.0 %collective-permute-start.3 = (bf16[96,1152]{1,0:T(8,128)(2,1)S(1)}, bf16[96,1152]{1,0:T(8,128)(2,1)S(1)}, u32[]{:S(2)}, u32[]{:S(2)}) collective-permute-start(bf16[96,1152]{1,0:T(8,128)(2,1)S(1)} %get-tuple-element.29.texts1), channel_id=1, source_target_pairs={{0,192},{24,216},{48,240},{72,264},{96,288},{120,312},{144,336},{1... | collective-permute-start | bytes 663560 | tf_op jit(solution)/shard_map/ppermute | solution.py:245
  26.8 1.5 %collective-permute-done.2.images2 = bf16[96,1152]{1,0:T(8,128)(2,1)S(1)} collective-permute-done((bf16[96,1152]{1,0:T(8,128)(2,1)S(1)}, bf16[96,1152]{1,0:T(8,128)(2,1)S(1)}, u32[]{:S(2)}, u32[]{:S(2)}) %collective-permute-start.2) | collective-permute-done | bytes 221216 | tf_op jit(solution)/shard_map/ppermute | solution.py:245
  28.3 2.6 %collective-permute-done.3.texts2 = bf16[96,1152]{1,0:T(8,128)(2,1)S(1)} collective-permute-done((bf16[96,1152]{1,0:T(8,128)(2,1)S(1)}, bf16[96,1152]{1,0:T(8,128)(2,1)S(1)}, u32[]{:S(2)}, u32[]{:S(2)}) %collective-permute-start.3) | collective-permute-done | bytes 221216 | tf_op jit(solution)/shard_map/ppermute | solution.py:245
  31.0 4.2 %collective-permute-start.4 = (bf16[192,1152]{1,0:T(8,128)(2,1)S(1)}, bf16[192,1152]{1,0:T(8,128)(2,1)S(1)}, u32[]{:S(2)}, u32[]{:S(2)}) collective-permute-start(bf16[192,1152]{1,0:T(8,128)(2,1)S(1)} %get-tuple-element.30.refs_2_), channel_id=1, source_target_pairs={{0,24},{24,0},{48,72},{72,48},{96,120},{120,96},{144,168},{168,144... | collective-permute-start | bytes 1327112 | tf_op jit(solution)/shard_map/ppermute | solution.py:248
  36.6 11.8 %collective-permute-start.7 = (bf16[48,1280]{1,0:T(8,128)(2,1)S(1)}, bf16[48,1280]{1,0:T(8,128)(2,1)S(1)}, u32[]{:S(2)}, u32[]{:S(2)}) collective-permute-start(bf16[48,1280]{1,0:T(8,128)(2,1)S(1)} %get-tuple-element.37), channel_id=1, source_target_pairs={{0,8},{1,9},{2,10},{3,11},{4,12},{5,13},{6,14},{7,15},{8,16},{9,17... | collective-permute-start | bytes 368648 | tf_op jit(solution)/shard_map/ppermute | solution.py:236
  48.5 1.9 %collective-permute-start.8 = (bf16[48,1280]{1,0:T(8,128)(2,1)S(1)}, bf16[48,1280]{1,0:T(8,128)(2,1)S(1)}, u32[]{:S(2)}, u32[]{:S(2)}) collective-permute-start(bf16[48,1280]{1,0:T(8,128)(2,1)S(1)} %get-tuple-element.38), channel_id=1, source_target_pairs={{0,16},{1,17},{2,18},{3,19},{4,20},{5,21},{6,22},{7,23},{8,0},{9,1... | collective-permute-start | bytes 368648 | tf_op jit(solution)/shard_map/ppermute | solution.py:237
  51.7 2.3 %shard_map.113 = (f32[192,1280]{1,0:T(8,128)S(1)}, bf16[192,1280]{1,0:T(8,128)(2,1)}, f32[96,1152]{1,0:T(8,128)S(1)}, bf16[96,1152]{1,0:T(8,128)(2,1)}) custom-call(f32[1]{0:T(128)S(6)} %copy.15.refs_0_.scale_ref, f32[1]{0:T(128)S(6)} %copy.16.refs_1_.bias_ref, bf16[192,1152]{1,0:T(8,128)(2,1)S(1)} %get-tuple-element.30.refs_2_, ...), custom_call_target="tpu_custom_call" | custom-call | tf_op jit(solution)/shard_map/pallas_call | solution.py:46
  54.1 3.1 %collective-permute-start.6 = (bf16[96,1152]{1,0:T(8,128)(2,1)}, bf16[96,1152]{1,0:T(8,128)(2,1)}, u32[]{:S(2)}, u32[]{:S(2)}) collective-permute-start(bf16[96,1152]{1,0:T(8,128)(2,1)} %get-tuple-element.35), channel_id=1, source_target_pairs={{0,192},{24,216},{48,240},{72,264},{96,288},{120,312},{144,336},{1... | collective-permute-start | bytes 663560 | tf_op jit(solution)/shard_map/ppermute | solution.py:256
  57.2 2.5 %collective-permute-start.5 = (bf16[192,1280]{1,0:T(8,128)(2,1)}, bf16[192,1280]{1,0:T(8,128)(2,1)}, u32[]{:S(2)}, u32[]{:S(2)}) collective-permute-start(bf16[192,1280]{1,0:T(8,128)(2,1)} %get-tuple-element.33), channel_id=1, source_target_pairs={{0,24},{24,0},{48,72},{72,48},{96,120},{120,96},{144,168},{168,144... | collective-permute-start | bytes 1474568 | tf_op jit(solution)/shard_map/ppermute | solution.py:255
  59.7 3.6 %shard_map.115 = (bf16[8,3,16,1152]{3,2,1,0:T(8,128)(2,1)}, f32[48,1280]{1,0:T(8,128)S(1)}, bf16[48,1280]{1,0:T(8,128)(2,1)S(1)}, bf16[48,1280]{1,0:T(8,128)(2,1)S(1)}) custom-call(s32[2]{0:T(128)S(1)} %pad_add_fusion.1.zh_ref, f32[1]{0:T(128)S(6)} %copy.15.refs_0_.scale_ref, f32[1]{0:T(128)S(6)} %copy.16.refs_1_.bias_ref, ...), custom_call_target="tpu_custom_call" | custom-call | flops 199999995904 | tf_op jit(solution)/shard_map/pallas_call | solution.py:46
  63.3 6.3 %collective-permute-start.9 = (bf16[48,1280]{1,0:T(8,128)(2,1)S(1)}, bf16[48,1280]{1,0:T(8,128)(2,1)S(1)}, u32[]{:S(2)}, u32[]{:S(2)}) collective-permute-start(bf16[48,1280]{1,0:T(8,128)(2,1)S(1)} %get-tuple-element.39), channel_id=1, source_target_pairs={{0,16},{1,17},{2,18},{3,19},{4,20},{5,21},{6,22},{7,23},{8,0},{9,1... | collective-permute-start | bytes 368648 | tf_op jit(solution)/shard_map/ppermute | solution.py:264
  69.6 6.7 %all-to-all-start.1 = ((bf16[8,48,1152]{2,1,0:T(8,128)(2,1)}), bf16[8,48,1152]{2,1,0:T(8,128)(2,1)}, u32[]{:S(2)}, u32[]{:S(2)}) async-start(bf16[8,48,1152]{2,1,0:T(8,128)(2,1)} %bitcast.6), calls=%async_computation.1 | async-start | bytes 1769472 | tf_op jit(solution)/shard_map/all_to_all | solution.py:232
  76.4 1.4 %shard_map.116 = (f32[96,1280]{1,0:T(8,128)S(1)}, bf16[96,1280]{1,0:T(8,128)(2,1)S(1)}, f32[48,1152]{1,0:T(8,128)S(1)}, bf16[48,1152]{1,0:T(8,128)(2,1)S(1)}) custom-call(f32[192,1280]{1,0:T(8,128)S(1)} %get-tuple-element.32.own, bf16[192,1280]{1,0:T(8,128)(2,1)} %collective-permute-done.5.got, f32[96,1152]{1,0:T(8,128)S(1)} %get-tuple-element.34.own_text, ...), custom_call_target="tpu_custom_call" | custom-call | flops 199999995904 | tf_op jit(solution)/shard_map/pallas_call | solution.py:46
  77.8 3.4 %collective-permute-start.10 = (bf16[96,1280]{1,0:T(8,128)(2,1)S(1)}, bf16[96,1280]{1,0:T(8,128)(2,1)S(1)}, u32[]{:S(2)}, u32[]{:S(2)}) collective-permute-start(bf16[96,1280]{1,0:T(8,128)(2,1)S(1)} %get-tuple-element.41), channel_id=1, source_target_pairs={{0,48},{24,72},{48,0},{72,24},{96,144},{120,168},{144,96},{168,120... | collective-permute-start | bytes 737288 | tf_op jit(solution)/shard_map/ppermute | solution.py:272
  81.3 4.3 %collective-permute-start.11 = (bf16[48,1152]{1,0:T(8,128)(2,1)S(1)}, bf16[48,1152]{1,0:T(8,128)(2,1)S(1)}, u32[]{:S(2)}, u32[]{:S(2)}) collective-permute-start(bf16[48,1152]{1,0:T(8,128)(2,1)S(1)} %get-tuple-element.43), channel_id=1, source_target_pairs={{0,384},{24,408},{48,432},{72,456},{96,480},{120,504},{144,528},{1... | collective-permute-start | bytes 331784 | tf_op jit(solution)/shard_map/ppermute | solution.py:273
  85.6 5.5 %collective-permute-start.13 = (bf16[48,1280]{1,0:T(8,128)(2,1)S(1)}, bf16[48,1280]{1,0:T(8,128)(2,1)S(1)}, u32[]{:S(2)}, u32[]{:S(2)}) collective-permute-start(bf16[48,1280]{1,0:T(8,128)(2,1)S(1)} %get-tuple-element.47), channel_id=1, source_target_pairs={{0,8},{1,9},{2,10},{3,11},{4,12},{5,13},{6,14},{7,15},{8,16},{9,17... | collective-permute-start | bytes 368648 | tf_op jit(solution)/shard_map/ppermute | solution.py:265
  92.0 2.1 %collective-permute-start.12 = (bf16[48,1280]{1,0:T(8,128)(2,1)S(1)}, bf16[48,1280]{1,0:T(8,128)(2,1)S(1)}, u32[]{:S(2)}, u32[]{:S(2)}) collective-permute-start(bf16[48,1280]{1,0:T(8,128)(2,1)S(1)} %get-tuple-element.45), channel_id=1, source_target_pairs={{0,144},{24,168},{48,96},{72,120},{96,48},{120,72},{144,0},{168,24... | collective-permute-start | bytes 368648 | tf_op jit(solution)/shard_map/ppermute | solution.py:278
  94.1 8.1 %all-to-all-done.1 = bf16[8,48,1152]{2,1,0:T(8,128)(2,1)} async-done(((bf16[8,48,1152]{2,1,0:T(8,128)(2,1)}), bf16[8,48,1152]{2,1,0:T(8,128)(2,1)}, u32[]{:S(2)}, u32[]{:S(2)}) %all-to-all-start.1) | async-done | bytes 884768 | tf_op jit(solution)/shard_map/all_to_all | solution.py:232
  102.2 1.2 %copy.14 = bf16[3,8,16,1152]{3,2,1,0:T(8,128)(2,1)S(1)} copy(bf16[3,8,16,1152]{3,2,0,1:T(8,128)(2,1)} %bitcast.8) | data formatting | bytes 1769472 | tf_op jit(solution)/shard_map/transpose | solution.py:279
  (33 shorter events, 3.4 us)
Async XLA Ops:
  0.6 20.2 %collective-permute-start.1 = (bf16[48,1152]{1,0:T(8,128)(2,1)}, bf16[48,1152]{1,0:T(8,128)(2,1)S(1)}, u32[]{:S(2)}, u32[]{:S(2)}) collective-permute-start(bf16[48,1152]{1,0:T(8,128)(2,1)} %text.1), channel_id=1, source_target_pairs={{0,384},{24,408},{48,432},{72,456},{96,480},{120,504},{144,528},{1... | collective-permute-start | bytes 331784 | tf_op jit(solution)/shard_map/ppermute | solution.py:241
  7.3 13.5 %collective-permute-start = (bf16[48,1152]{1,0:T(8,128)(2,1)}, bf16[48,1152]{1,0:T(8,128)(2,1)S(1)}, u32[]{:S(2)}, u32[]{:S(2)}) collective-permute-start(bf16[48,1152]{1,0:T(8,128)(2,1)} %image.5), channel_id=1, source_target_pairs={{0,144},{24,168},{48,96},{72,120},{96,48},{120,72},{144,0},{168,24... | collective-permute-start | bytes 331784 | tf_op jit(solution)/shard_map/ppermute | solution.py:241
  13.8 7.0 %copy-start.1 = (bf16[48,1152]{1,0:T(8,128)(2,1)S(1)}, bf16[48,1152]{1,0:T(8,128)(2,1)}, u32[]{:S(2)}) copy-start(bf16[48,1152]{1,0:T(8,128)(2,1)} %image.5) | copy-start | bytes 331780
  13.8 7.0 %copy-start.2 = (bf16[48,1152]{1,0:T(8,128)(2,1)S(1)}, bf16[48,1152]{1,0:T(8,128)(2,1)}, u32[]{:S(2)}) copy-start(bf16[48,1152]{1,0:T(8,128)(2,1)} %text.1) | copy-start | bytes 331780
  13.8 45.8 %all-to-all-start = ((bf16[8,48,1152]{2,1,0:T(8,128)(2,1)}), bf16[8,48,1152]{2,1,0:T(8,128)(2,1)}, u32[]{:S(2)}, u32[]{:S(2)}) async-start(bf16[8,48,1152]{2,1,0:T(8,128)(2,1)} %bitcast.4), calls=%async_computation | async-start | bytes 1769472 | tf_op jit(solution)/shard_map/all_to_all | solution.py:232
  20.9 7.4 %collective-permute-start.2 = (bf16[96,1152]{1,0:T(8,128)(2,1)S(1)}, bf16[96,1152]{1,0:T(8,128)(2,1)S(1)}, u32[]{:S(2)}, u32[]{:S(2)}) collective-permute-start(bf16[96,1152]{1,0:T(8,128)(2,1)S(1)} %get-tuple-element.28.images1), channel_id=1, source_target_pairs={{0,48},{24,72},{48,0},{72,24},{96,144},{120,168},{144,96},{168,120... | collective-permute-start | bytes 663560 | tf_op jit(solution)/shard_map/ppermute | solution.py:245
  22.8 8.1 %collective-permute-start.3 = (bf16[96,1152]{1,0:T(8,128)(2,1)S(1)}, bf16[96,1152]{1,0:T(8,128)(2,1)S(1)}, u32[]{:S(2)}, u32[]{:S(2)}) collective-permute-start(bf16[96,1152]{1,0:T(8,128)(2,1)S(1)} %get-tuple-element.29.texts1), channel_id=1, source_target_pairs={{0,192},{24,216},{48,240},{72,264},{96,288},{120,312},{144,336},{1... | collective-permute-start | bytes 663560 | tf_op jit(solution)/shard_map/ppermute | solution.py:245
  31.0 20.7 %collective-permute-start.4 = (bf16[192,1152]{1,0:T(8,128)(2,1)S(1)}, bf16[192,1152]{1,0:T(8,128)(2,1)S(1)}, u32[]{:S(2)}, u32[]{:S(2)}) collective-permute-start(bf16[192,1152]{1,0:T(8,128)(2,1)S(1)} %get-tuple-element.30.refs_2_), channel_id=1, source_target_pairs={{0,24},{24,0},{48,72},{72,48},{96,120},{120,96},{144,168},{168,144... | collective-permute-start | bytes 1327112 | tf_op jit(solution)/shard_map/ppermute | solution.py:248
  35.2 0.7 copy-start.4
  35.2 0.7 copy-start.3
  35.2 0.7 copy-start.5
  36.6 23.0 %collective-permute-start.7 = (bf16[48,1280]{1,0:T(8,128)(2,1)S(1)}, bf16[48,1280]{1,0:T(8,128)(2,1)S(1)}, u32[]{:S(2)}, u32[]{:S(2)}) collective-permute-start(bf16[48,1280]{1,0:T(8,128)(2,1)S(1)} %get-tuple-element.37), channel_id=1, source_target_pairs={{0,8},{1,9},{2,10},{3,11},{4,12},{5,13},{6,14},{7,15},{8,16},{9,17... | collective-permute-start | bytes 368648 | tf_op jit(solution)/shard_map/ppermute | solution.py:236
  48.5 11.2 %collective-permute-start.8 = (bf16[48,1280]{1,0:T(8,128)(2,1)S(1)}, bf16[48,1280]{1,0:T(8,128)(2,1)S(1)}, u32[]{:S(2)}, u32[]{:S(2)}) collective-permute-start(bf16[48,1280]{1,0:T(8,128)(2,1)S(1)} %get-tuple-element.38), channel_id=1, source_target_pairs={{0,16},{1,17},{2,18},{3,19},{4,20},{5,21},{6,22},{7,23},{8,0},{9,1... | collective-permute-start | bytes 368648 | tf_op jit(solution)/shard_map/ppermute | solution.py:237
  54.1 22.3 %collective-permute-start.6 = (bf16[96,1152]{1,0:T(8,128)(2,1)}, bf16[96,1152]{1,0:T(8,128)(2,1)}, u32[]{:S(2)}, u32[]{:S(2)}) collective-permute-start(bf16[96,1152]{1,0:T(8,128)(2,1)} %get-tuple-element.35), channel_id=1, source_target_pairs={{0,192},{24,216},{48,240},{72,264},{96,288},{120,312},{144,336},{1... | collective-permute-start | bytes 663560 | tf_op jit(solution)/shard_map/ppermute | solution.py:256
  57.2 19.2 %collective-permute-start.5 = (bf16[192,1280]{1,0:T(8,128)(2,1)}, bf16[192,1280]{1,0:T(8,128)(2,1)}, u32[]{:S(2)}, u32[]{:S(2)}) collective-permute-start(bf16[192,1280]{1,0:T(8,128)(2,1)} %get-tuple-element.33), channel_id=1, source_target_pairs={{0,24},{24,0},{48,72},{72,48},{96,120},{120,96},{144,168},{168,144... | collective-permute-start | bytes 1474568 | tf_op jit(solution)/shard_map/ppermute | solution.py:255
  63.3 13.1 %collective-permute-start.9 = (bf16[48,1280]{1,0:T(8,128)(2,1)S(1)}, bf16[48,1280]{1,0:T(8,128)(2,1)S(1)}, u32[]{:S(2)}, u32[]{:S(2)}) collective-permute-start(bf16[48,1280]{1,0:T(8,128)(2,1)S(1)} %get-tuple-element.39), channel_id=1, source_target_pairs={{0,16},{1,17},{2,18},{3,19},{4,20},{5,21},{6,22},{7,23},{8,0},{9,1... | collective-permute-start | bytes 368648 | tf_op jit(solution)/shard_map/ppermute | solution.py:264
  69.6 32.5 %all-to-all-start.1 = ((bf16[8,48,1152]{2,1,0:T(8,128)(2,1)}), bf16[8,48,1152]{2,1,0:T(8,128)(2,1)}, u32[]{:S(2)}, u32[]{:S(2)}) async-start(bf16[8,48,1152]{2,1,0:T(8,128)(2,1)} %bitcast.6), calls=%async_computation.1 | async-start | bytes 1769472 | tf_op jit(solution)/shard_map/all_to_all | solution.py:232
  77.8 13.3 %collective-permute-start.10 = (bf16[96,1280]{1,0:T(8,128)(2,1)S(1)}, bf16[96,1280]{1,0:T(8,128)(2,1)S(1)}, u32[]{:S(2)}, u32[]{:S(2)}) collective-permute-start(bf16[96,1280]{1,0:T(8,128)(2,1)S(1)} %get-tuple-element.41), channel_id=1, source_target_pairs={{0,48},{24,72},{48,0},{72,24},{96,144},{120,168},{144,96},{168,120... | collective-permute-start | bytes 737288 | tf_op jit(solution)/shard_map/ppermute | solution.py:272
  81.3 9.8 %collective-permute-start.11 = (bf16[48,1152]{1,0:T(8,128)(2,1)S(1)}, bf16[48,1152]{1,0:T(8,128)(2,1)S(1)}, u32[]{:S(2)}, u32[]{:S(2)}) collective-permute-start(bf16[48,1152]{1,0:T(8,128)(2,1)S(1)} %get-tuple-element.43), channel_id=1, source_target_pairs={{0,384},{24,408},{48,432},{72,456},{96,480},{120,504},{144,528},{1... | collective-permute-start | bytes 331784 | tf_op jit(solution)/shard_map/ppermute | solution.py:273
  85.6 17.8 %collective-permute-start.13 = (bf16[48,1280]{1,0:T(8,128)(2,1)S(1)}, bf16[48,1280]{1,0:T(8,128)(2,1)S(1)}, u32[]{:S(2)}, u32[]{:S(2)}) collective-permute-start(bf16[48,1280]{1,0:T(8,128)(2,1)S(1)} %get-tuple-element.47), channel_id=1, source_target_pairs={{0,8},{1,9},{2,10},{3,11},{4,12},{5,13},{6,14},{7,15},{8,16},{9,17... | collective-permute-start | bytes 368648 | tf_op jit(solution)/shard_map/ppermute | solution.py:265
  92.0 11.5 %collective-permute-start.12 = (bf16[48,1280]{1,0:T(8,128)(2,1)S(1)}, bf16[48,1280]{1,0:T(8,128)(2,1)S(1)}, u32[]{:S(2)}, u32[]{:S(2)}) collective-permute-start(bf16[48,1280]{1,0:T(8,128)(2,1)S(1)} %get-tuple-element.45), channel_id=1, source_target_pairs={{0,144},{24,168},{48,96},{72,120},{96,48},{120,72},{144,0},{168,24... | collective-permute-start | bytes 368648 | tf_op jit(solution)/shard_map/ppermute | solution.py:278
  103.4 1.0 copy-start

commit v5 on v4

--- a/solution.py
+++ b/solution.py
@@ -19,16 +19,19 @@
 
 
 def partners(zl_bits, x_bits, c_bits):
+    zl_of = zl_bits if isinstance(zl_bits, tuple) else (zl_bits,) * N_C
+
     def blk_of(zl, x, c):
         return (zl * N_X + x) * N_C + c
 
     return [
-        (blk_of(z, x, c), blk_of(z ^ zl_bits, x ^ x_bits, c ^ c_bits))
+        (blk_of(z, x, c), blk_of(z ^ zl_of[c], x ^ x_bits, c ^ c_bits))
         for z in range(N_ZL) for x in range(N_X) for c in range(N_C)
     ]
 
 
 ZL_NEAR, ZL_FAR = partners(1, 0, 0), partners(2, 0, 0)
+ZL_FIRST, ZL_LAST = partners((1, 2), 0, 0), partners((2, 1), 0, 0)
 X_NEAR, X_FAR = partners(0, 1, 0), partners(0, 3, 0)
 OTHER_CORE = partners(0, 0, 1)
 Y_GROUPS = [[h * N_Y + y for y in range(N_Y)] for h in range(N_ZH)]
@@ -124,7 +127,7 @@
         out[rows:, :] = second[...]
 
 
-def pairs(scale_ref, bias_ref, near_images, far_images, texts, keep, send, keep_text, send_text, rows):
+def pairs(place_ref, scale_ref, bias_ref, near_images, far_images, texts, keep, send, keep_text, send_text, rows):
     width = texts.shape[1]
     half = texts.shape[0] // 2
     sums = None
@@ -150,8 +153,12 @@
             send[:, :width] = grad.astype(BF16)
             send[:, width:] = split_lanes(extra)
             sums = sums + more
-    keep_text[...] = sums[:half]
-    send_text[...] = sums[half:].astype(BF16)
+    first = place_ref[1] > 0
+    far, near = sums[rows:half], sums[half:half + rows]
+    keep_text[:rows, :] = sums[:rows]
+    keep_text[rows:, :] = jnp.where(first, far, near)
+    send_text[:rows, :] = jnp.where(first, near, far).astype(BF16)
+    send_text[rows:, :] = sums[half + rows:].astype(BF16)
 
 
 def fold_tagged(own, got, keep, send):
@@ -250,10 +257,10 @@
     keep, send, keep_t, send_t = call(
         lambda *refs: pairs(*refs, rows=rows),
         [((n_i // 2, wide), F32), ((n_i // 2, wide), BF16), ((n_t // 2, width), F32), ((n_t // 2, width), BF16)],
-        (logit_scale, logit_bias, images, others, texts), [SMEM, SMEM] + [VMEM] * 3,
+        (zh, logit_scale, logit_bias, images, others, texts), [SMEM] * 3 + [VMEM] * 3,
     )
     got = lax.ppermute(send, "blk", OTHER_CORE)
-    got_t = lax.ppermute(send_t, "blk", ZL_NEAR)
+    got_t = lax.ppermute(send_t, "blk", ZL_FIRST)
 
     back, cap_own, send1, send2 = call(
         captions,
@@ -270,7 +277,7 @@
         (keep, got, keep_t, got_t, cap1), [VMEM] * 5, flops=FOLD,
     )
     got = lax.ppermute(send, "blk", X_NEAR)
-    got_t = lax.ppermute(send_t, "blk", ZL_FAR)
+    got_t = lax.ppermute(send_t, "blk", ZL_LAST)
     keep, send, text_grad = call(
         fold_last, [((rows, wide), F32), ((rows, wide), BF16), ((rows, width), F32)],
         (logit_scale, keep, got, keep_t, got_t), [SMEM] + [VMEM] * 4, flops=FOLD2,

time: 105 us -> 106 us (level)
  starting transfers between devices: 75.8 us -> 74.3 us
  waiting for transfers between devices: 12.2 us -> 13.7 us
    ppermute x2, starting transfers between devices: 7.37 us -> 4.08 us  [the longest x1 2.16 us: shards(): got_t = lax.ppermute(send_t, 'blk', ZL_FIRST)]
    all_to_all x2, waiting for transfers between devices: 8.11 us -> 9.59 us  [to_y(): x = lax.all_to_all(x, 'cap', 0, 0, axis_index_groups=Y_GROUPS, tiled=True)]
where the time goes in v5:
time: 106 us; the launch traced here: 105 us
  starting transfers between devices  74.3 us (70%)
  waiting for transfers between devices  13.7 us (13%)
  Pallas kernels  10.4 us (10%)
  local copies, waits for them, and re-layouts  4.19 us (4%)
  between operations  2.26 us (2%)
    all_to_all x2, starting transfers between devices, to_y(): x = lax.all_to_all(x, 'cap', 0, 0, axis_index_groups=Y_GROUPS, tiled=True)  13.7 us
    ppermute x1, starting transfers between devices, shards(): from1 = lax.ppermute(tag1, ('blk', 'cap'), shift_zh(1))  11.8 us
    pallas_call x8, Pallas kernels, call(): pl.pallas_call(body, out_shape=tuple((jax.ShapeDtypeStruct(s, d) for s, d...  10.4 us
    all_to_all x2, waiting for transfers between devices, to_y(): x = lax.all_to_all(x, 'cap', 0, 0, axis_index_groups=Y_GROUPS, tiled=True)  9.59 us
    ppermute x1, starting transfers between devices, shards(): lax.ppermute(text, 'blk', ZL_FAR)  6.64 us
    ppermute x1, starting transfers between devices, shards(): cap2 = lax.ppermute(send2, ('blk', 'cap'), shift_zh(-2))  6.38 us
    ppermute x1, starting transfers between devices, shards(): cap1 = lax.ppermute(send1, ('blk', 'cap'), shift_zh(-1))  6.3 us
    ppermute x1, starting transfers between devices, shards(): lax.ppermute(image, 'blk', X_FAR)  4.39 us
  transfers between devices with their start and end apart: 16, of which 3 were waited for; matrix products, arithmetic and copies ran while one was open for 3% of the time, Pallas kernels for 9%

profile of v5, /device:TPU:1, one launch (start us, length us, event | category | flops | bytes accessed | tf_op | source)
XLA Modules:
  0.0 104.9 jit_solution(13921516514038542073)
XLA Ops:
  0.6 6.6 %collective-permute-start.1 = (bf16[48,1152]{1,0:T(8,128)(2,1)}, bf16[48,1152]{1,0:T(8,128)(2,1)S(1)}, u32[]{:S(2)}, u32[]{:S(2)}) collective-permute-start(bf16[48,1152]{1,0:T(8,128)(2,1)} %text.1), channel_id=1, source_target_pairs={{0,384},{24,408},{48,432},{72,456},{96,480},{120,504},{144,528},{1... | collective-permute-start | bytes 331784 | tf_op jit(solution)/shard_map/ppermute | solution.py:248
  7.3 4.4 %collective-permute-start = (bf16[48,1152]{1,0:T(8,128)(2,1)}, bf16[48,1152]{1,0:T(8,128)(2,1)S(1)}, u32[]{:S(2)}, u32[]{:S(2)}) collective-permute-start(bf16[48,1152]{1,0:T(8,128)(2,1)} %image.5), channel_id=1, source_target_pairs={{0,144},{24,168},{48,96},{72,120},{96,48},{120,72},{144,0},{168,24... | collective-permute-start | bytes 331784 | tf_op jit(solution)/shard_map/ppermute | solution.py:248
  11.7 2.1 %copy.13 = bf16[8,3,16,1152]{3,2,1,0:T(8,128)(2,1)} copy(bf16[8,3,16,1152]{3,2,0,1:T(8,128)(2,1)} %bitcast.15) | data formatting | bytes 1769472 | tf_op jit(solution)/shard_map/transpose | solution.py:242
  13.8 7.0 %all-to-all-start = ((bf16[8,48,1152]{2,1,0:T(8,128)(2,1)}), bf16[8,48,1152]{2,1,0:T(8,128)(2,1)}, u32[]{:S(2)}, u32[]{:S(2)}) async-start(bf16[8,48,1152]{2,1,0:T(8,128)(2,1)} %bitcast.4), calls=%async_computation | async-start | bytes 1769472 | tf_op jit(solution)/shard_map/all_to_all | solution.py:239
  20.9 1.9 %collective-permute-start.2 = (bf16[96,1152]{1,0:T(8,128)(2,1)S(1)}, bf16[96,1152]{1,0:T(8,128)(2,1)S(1)}, u32[]{:S(2)}, u32[]{:S(2)}) collective-permute-start(bf16[96,1152]{1,0:T(8,128)(2,1)S(1)} %get-tuple-element.28.images1), channel_id=1, source_target_pairs={{0,48},{24,72},{48,0},{72,24},{96,144},{120,168},{144,96},{168,120... | collective-permute-start | bytes 663560 | tf_op jit(solution)/shard_map/ppermute | solution.py:252
  22.8 4.0 %collective-permute-start.3 = (bf16[96,1152]{1,0:T(8,128)(2,1)S(1)}, bf16[96,1152]{1,0:T(8,128)(2,1)S(1)}, u32[]{:S(2)}, u32[]{:S(2)}) collective-permute-start(bf16[96,1152]{1,0:T(8,128)(2,1)S(1)} %get-tuple-element.29.texts1), channel_id=1, source_target_pairs={{0,192},{24,216},{48,240},{72,264},{96,288},{120,312},{144,336},{1... | collective-permute-start | bytes 663560 | tf_op jit(solution)/shard_map/ppermute | solution.py:252
  26.8 1.5 %collective-permute-done.2.images2 = bf16[96,1152]{1,0:T(8,128)(2,1)S(1)} collective-permute-done((bf16[96,1152]{1,0:T(8,128)(2,1)S(1)}, bf16[96,1152]{1,0:T(8,128)(2,1)S(1)}, u32[]{:S(2)}, u32[]{:S(2)}) %collective-permute-start.2) | collective-permute-done | bytes 221216 | tf_op jit(solution)/shard_map/ppermute | solution.py:252
  28.3 2.6 %collective-permute-done.3.texts2 = bf16[96,1152]{1,0:T(8,128)(2,1)S(1)} collective-permute-done((bf16[96,1152]{1,0:T(8,128)(2,1)S(1)}, bf16[96,1152]{1,0:T(8,128)(2,1)S(1)}, u32[]{:S(2)}, u32[]{:S(2)}) %collective-permute-start.3) | collective-permute-done | bytes 221216 | tf_op jit(solution)/shard_map/ppermute | solution.py:252
  31.0 4.2 %collective-permute-start.4 = (bf16[192,1152]{1,0:T(8,128)(2,1)S(1)}, bf16[192,1152]{1,0:T(8,128)(2,1)S(1)}, u32[]{:S(2)}, u32[]{:S(2)}) collective-permute-start(bf16[192,1152]{1,0:T(8,128)(2,1)S(1)} %get-tuple-element.30.refs_3_), channel_id=1, source_target_pairs={{0,24},{24,0},{48,72},{72,48},{96,120},{120,96},{144,168},{168,144... | collective-permute-start | bytes 1327112 | tf_op jit(solution)/shard_map/ppermute | solution.py:255
  36.6 11.8 %collective-permute-start.7 = (bf16[48,1280]{1,0:T(8,128)(2,1)S(1)}, bf16[48,1280]{1,0:T(8,128)(2,1)S(1)}, u32[]{:S(2)}, u32[]{:S(2)}) collective-permute-start(bf16[48,1280]{1,0:T(8,128)(2,1)S(1)} %get-tuple-element.37), channel_id=1, source_target_pairs={{0,8},{1,9},{2,10},{3,11},{4,12},{5,13},{6,14},{7,15},{8,16},{9,17... | collective-permute-start | bytes 368648 | tf_op jit(solution)/shard_map/ppermute | solution.py:243
  48.5 1.9 %collective-permute-start.8 = (bf16[48,1280]{1,0:T(8,128)(2,1)S(1)}, bf16[48,1280]{1,0:T(8,128)(2,1)S(1)}, u32[]{:S(2)}, u32[]{:S(2)}) collective-permute-start(bf16[48,1280]{1,0:T(8,128)(2,1)S(1)} %get-tuple-element.38), channel_id=1, source_target_pairs={{0,16},{1,17},{2,18},{3,19},{4,20},{5,21},{6,22},{7,23},{8,0},{9,1... | collective-permute-start | bytes 368648 | tf_op jit(solution)/shard_map/ppermute | solution.py:244
  51.7 2.9 %shard_map.113 = (f32[192,1280]{1,0:T(8,128)S(1)}, bf16[192,1280]{1,0:T(8,128)(2,1)}, f32[96,1152]{1,0:T(8,128)S(1)}, bf16[96,1152]{1,0:T(8,128)(2,1)}) custom-call(s32[2]{0:T(128)S(1)} %pad_add_fusion.1.refs_0_.zh_ref, f32[1]{0:T(128)S(6)} %copy.15.refs_1_.scale_ref, f32[1]{0:T(128)S(6)} %copy.16.refs_2_.bias_ref, ...), custom_call_target="tpu_custom_call" | custom-call | tf_op jit(solution)/shard_map/pallas_call | solution.py:49
  54.6 2.2 %collective-permute-start.6 = (bf16[96,1152]{1,0:T(8,128)(2,1)}, bf16[96,1152]{1,0:T(8,128)(2,1)}, u32[]{:S(2)}, u32[]{:S(2)}) collective-permute-start(bf16[96,1152]{1,0:T(8,128)(2,1)} %get-tuple-element.35), channel_id=1, source_target_pairs={{0,192},{24,408},{48,240},{72,456},{96,288},{120,504},{144,336},{1... | collective-permute-start | bytes 663560 | tf_op jit(solution)/shard_map/ppermute | solution.py:263
  56.8 3.4 %collective-permute-start.5 = (bf16[192,1280]{1,0:T(8,128)(2,1)}, bf16[192,1280]{1,0:T(8,128)(2,1)}, u32[]{:S(2)}, u32[]{:S(2)}) collective-permute-start(bf16[192,1280]{1,0:T(8,128)(2,1)} %get-tuple-element.33), channel_id=1, source_target_pairs={{0,24},{24,0},{48,72},{72,48},{96,120},{120,96},{144,168},{168,144... | collective-permute-start | bytes 1474568 | tf_op jit(solution)/shard_map/ppermute | solution.py:262
  60.2 3.6 %shard_map.115 = (bf16[8,3,16,1152]{3,2,1,0:T(8,128)(2,1)}, f32[48,1280]{1,0:T(8,128)S(1)}, bf16[48,1280]{1,0:T(8,128)(2,1)S(1)}, bf16[48,1280]{1,0:T(8,128)(2,1)S(1)}) custom-call(s32[2]{0:T(128)S(1)} %pad_add_fusion.1.refs_0_.zh_ref, f32[1]{0:T(128)S(6)} %copy.15.refs_1_.scale_ref, f32[1]{0:T(128)S(6)} %copy.16.refs_2_.bias_ref, ...), custom_call_target="tpu_custom_call" | custom-call | flops 199999995904 | tf_op jit(solution)/shard_map/pallas_call | solution.py:49
  63.9 6.3 %collective-permute-start.9 = (bf16[48,1280]{1,0:T(8,128)(2,1)S(1)}, bf16[48,1280]{1,0:T(8,128)(2,1)S(1)}, u32[]{:S(2)}, u32[]{:S(2)}) collective-permute-start(bf16[48,1280]{1,0:T(8,128)(2,1)S(1)} %get-tuple-element.39), channel_id=1, source_target_pairs={{0,16},{1,17},{2,18},{3,19},{4,20},{5,21},{6,22},{7,23},{8,0},{9,1... | collective-permute-start | bytes 368648 | tf_op jit(solution)/shard_map/ppermute | solution.py:271
  70.2 6.7 %all-to-all-start.1 = ((bf16[8,48,1152]{2,1,0:T(8,128)(2,1)}), bf16[8,48,1152]{2,1,0:T(8,128)(2,1)}, u32[]{:S(2)}, u32[]{:S(2)}) async-start(bf16[8,48,1152]{2,1,0:T(8,128)(2,1)} %bitcast.6), calls=%async_computation.1 | async-start | bytes 1769472 | tf_op jit(solution)/shard_map/all_to_all | solution.py:239
  76.9 1.4 %shard_map.116 = (f32[96,1280]{1,0:T(8,128)S(1)}, bf16[96,1280]{1,0:T(8,128)(2,1)S(1)}, f32[48,1152]{1,0:T(8,128)S(1)}, bf16[48,1152]{1,0:T(8,128)(2,1)S(1)}) custom-call(f32[192,1280]{1,0:T(8,128)S(1)} %get-tuple-element.32.own, bf16[192,1280]{1,0:T(8,128)(2,1)} %collective-permute-done.5.got, f32[96,1152]{1,0:T(8,128)S(1)} %get-tuple-element.34.own_text, ...), custom_call_target="tpu_custom_call" | custom-call | flops 199999995904 | tf_op jit(solution)/shard_map/pallas_call | solution.py:49
  78.4 3.4 %collective-permute-start.10 = (bf16[96,1280]{1,0:T(8,128)(2,1)S(1)}, bf16[96,1280]{1,0:T(8,128)(2,1)S(1)}, u32[]{:S(2)}, u32[]{:S(2)}) collective-permute-start(bf16[96,1280]{1,0:T(8,128)(2,1)S(1)} %get-tuple-element.41), channel_id=1, source_target_pairs={{0,48},{24,72},{48,0},{72,24},{96,144},{120,168},{144,96},{168,120... | collective-permute-start | bytes 737288 | tf_op jit(solution)/shard_map/ppermute | solution.py:279
  81.8 1.9 %collective-permute-start.11 = (bf16[48,1152]{1,0:T(8,128)(2,1)S(1)}, bf16[48,1152]{1,0:T(8,128)(2,1)S(1)}, u32[]{:S(2)}, u32[]{:S(2)}) collective-permute-start(bf16[48,1152]{1,0:T(8,128)(2,1)S(1)} %get-tuple-element.43), channel_id=1, source_target_pairs={{0,384},{24,216},{48,432},{72,264},{96,480},{120,312},{144,528},{1... | collective-permute-start | bytes 331784 | tf_op jit(solution)/shard_map/ppermute | solution.py:280
  83.8 6.4 %collective-permute-start.13 = (bf16[48,1280]{1,0:T(8,128)(2,1)S(1)}, bf16[48,1280]{1,0:T(8,128)(2,1)S(1)}, u32[]{:S(2)}, u32[]{:S(2)}) collective-permute-start(bf16[48,1280]{1,0:T(8,128)(2,1)S(1)} %get-tuple-element.47), channel_id=1, source_target_pairs={{0,8},{1,9},{2,10},{3,11},{4,12},{5,13},{6,14},{7,15},{8,16},{9,17... | collective-permute-start | bytes 368648 | tf_op jit(solution)/shard_map/ppermute | solution.py:272
  91.0 2.1 %collective-permute-start.12 = (bf16[48,1280]{1,0:T(8,128)(2,1)S(1)}, bf16[48,1280]{1,0:T(8,128)(2,1)S(1)}, u32[]{:S(2)}, u32[]{:S(2)}) collective-permute-start(bf16[48,1280]{1,0:T(8,128)(2,1)S(1)} %get-tuple-element.45), channel_id=1, source_target_pairs={{0,144},{24,168},{48,96},{72,120},{96,48},{120,72},{144,0},{168,24... | collective-permute-start | bytes 368648 | tf_op jit(solution)/shard_map/ppermute | solution.py:285
  93.1 9.6 %all-to-all-done.1 = bf16[8,48,1152]{2,1,0:T(8,128)(2,1)} async-done(((bf16[8,48,1152]{2,1,0:T(8,128)(2,1)}), bf16[8,48,1152]{2,1,0:T(8,128)(2,1)}, u32[]{:S(2)}, u32[]{:S(2)}) %all-to-all-start.1) | async-done | bytes 884768 | tf_op jit(solution)/shard_map/all_to_all | solution.py:239
  102.7 1.2 %copy.14 = bf16[3,8,16,1152]{3,2,1,0:T(8,128)(2,1)S(1)} copy(bf16[3,8,16,1152]{3,2,0,1:T(8,128)(2,1)} %bitcast.8) | data formatting | bytes 1769472 | tf_op jit(solution)/shard_map/transpose | solution.py:286
  (33 shorter events, 3.4 us)
Async XLA Ops:
  0.6 20.2 %collective-permute-start.1 = (bf16[48,1152]{1,0:T(8,128)(2,1)}, bf16[48,1152]{1,0:T(8,128)(2,1)S(1)}, u32[]{:S(2)}, u32[]{:S(2)}) collective-permute-start(bf16[48,1152]{1,0:T(8,128)(2,1)} %text.1), channel_id=1, source_target_pairs={{0,384},{24,408},{48,432},{72,456},{96,480},{120,504},{144,528},{1... | collective-permute-start | bytes 331784 | tf_op jit(solution)/shard_map/ppermute | solution.py:248
  7.3 13.5 %collective-permute-start = (bf16[48,1152]{1,0:T(8,128)(2,1)}, bf16[48,1152]{1,0:T(8,128)(2,1)S(1)}, u32[]{:S(2)}, u32[]{:S(2)}) collective-permute-start(bf16[48,1152]{1,0:T(8,128)(2,1)} %image.5), channel_id=1, source_target_pairs={{0,144},{24,168},{48,96},{72,120},{96,48},{120,72},{144,0},{168,24... | collective-permute-start | bytes 331784 | tf_op jit(solution)/shard_map/ppermute | solution.py:248
  13.8 7.0 %copy-start.1 = (bf16[48,1152]{1,0:T(8,128)(2,1)S(1)}, bf16[48,1152]{1,0:T(8,128)(2,1)}, u32[]{:S(2)}) copy-start(bf16[48,1152]{1,0:T(8,128)(2,1)} %image.5) | copy-start | bytes 331780
  13.8 7.0 %copy-start.2 = (bf16[48,1152]{1,0:T(8,128)(2,1)S(1)}, bf16[48,1152]{1,0:T(8,128)(2,1)}, u32[]{:S(2)}) copy-start(bf16[48,1152]{1,0:T(8,128)(2,1)} %text.1) | copy-start | bytes 331780
  13.8 46.4 %all-to-all-start = ((bf16[8,48,1152]{2,1,0:T(8,128)(2,1)}), bf16[8,48,1152]{2,1,0:T(8,128)(2,1)}, u32[]{:S(2)}, u32[]{:S(2)}) async-start(bf16[8,48,1152]{2,1,0:T(8,128)(2,1)} %bitcast.4), calls=%async_computation | async-start | bytes 1769472 | tf_op jit(solution)/shard_map/all_to_all | solution.py:239
  20.9 7.4 %collective-permute-start.2 = (bf16[96,1152]{1,0:T(8,128)(2,1)S(1)}, bf16[96,1152]{1,0:T(8,128)(2,1)S(1)}, u32[]{:S(2)}, u32[]{:S(2)}) collective-permute-start(bf16[96,1152]{1,0:T(8,128)(2,1)S(1)} %get-tuple-element.28.images1), channel_id=1, source_target_pairs={{0,48},{24,72},{48,0},{72,24},{96,144},{120,168},{144,96},{168,120... | collective-permute-start | bytes 663560 | tf_op jit(solution)/shard_map/ppermute | solution.py:252
  22.8 8.1 %collective-permute-start.3 = (bf16[96,1152]{1,0:T(8,128)(2,1)S(1)}, bf16[96,1152]{1,0:T(8,128)(2,1)S(1)}, u32[]{:S(2)}, u32[]{:S(2)}) collective-permute-start(bf16[96,1152]{1,0:T(8,128)(2,1)S(1)} %get-tuple-element.29.texts1), channel_id=1, source_target_pairs={{0,192},{24,216},{48,240},{72,264},{96,288},{120,312},{144,336},{1... | collective-permute-start | bytes 663560 | tf_op jit(solution)/shard_map/ppermute | solution.py:252
  31.0 20.7 %collective-permute-start.4 = (bf16[192,1152]{1,0:T(8,128)(2,1)S(1)}, bf16[192,1152]{1,0:T(8,128)(2,1)S(1)}, u32[]{:S(2)}, u32[]{:S(2)}) collective-permute-start(bf16[192,1152]{1,0:T(8,128)(2,1)S(1)} %get-tuple-element.30.refs_3_), channel_id=1, source_target_pairs={{0,24},{24,0},{48,72},{72,48},{96,120},{120,96},{144,168},{168,144... | collective-permute-start | bytes 1327112 | tf_op jit(solution)/shard_map/ppermute | solution.py:255
  35.2 0.7 copy-start.4
  35.2 0.7 copy-start.3
  35.2 0.7 copy-start.5
  36.6 23.6 %collective-permute-start.7 = (bf16[48,1280]{1,0:T(8,128)(2,1)S(1)}, bf16[48,1280]{1,0:T(8,128)(2,1)S(1)}, u32[]{:S(2)}, u32[]{:S(2)}) collective-permute-start(bf16[48,1280]{1,0:T(8,128)(2,1)S(1)} %get-tuple-element.37), channel_id=1, source_target_pairs={{0,8},{1,9},{2,10},{3,11},{4,12},{5,13},{6,14},{7,15},{8,16},{9,17... | collective-permute-start | bytes 368648 | tf_op jit(solution)/shard_map/ppermute | solution.py:243
  48.5 11.7 %collective-permute-start.8 = (bf16[48,1280]{1,0:T(8,128)(2,1)S(1)}, bf16[48,1280]{1,0:T(8,128)(2,1)S(1)}, u32[]{:S(2)}, u32[]{:S(2)}) collective-permute-start(bf16[48,1280]{1,0:T(8,128)(2,1)S(1)} %get-tuple-element.38), channel_id=1, source_target_pairs={{0,16},{1,17},{2,18},{3,19},{4,20},{5,21},{6,22},{7,23},{8,0},{9,1... | collective-permute-start | bytes 368648 | tf_op jit(solution)/shard_map/ppermute | solution.py:244
  54.6 22.3 %collective-permute-start.6 = (bf16[96,1152]{1,0:T(8,128)(2,1)}, bf16[96,1152]{1,0:T(8,128)(2,1)}, u32[]{:S(2)}, u32[]{:S(2)}) collective-permute-start(bf16[96,1152]{1,0:T(8,128)(2,1)} %get-tuple-element.35), channel_id=1, source_target_pairs={{0,192},{24,408},{48,240},{72,456},{96,288},{120,504},{144,336},{1... | collective-permute-start | bytes 663560 | tf_op jit(solution)/shard_map/ppermute | solution.py:263
  56.8 20.2 %collective-permute-start.5 = (bf16[192,1280]{1,0:T(8,128)(2,1)}, bf16[192,1280]{1,0:T(8,128)(2,1)}, u32[]{:S(2)}, u32[]{:S(2)}) collective-permute-start(bf16[192,1280]{1,0:T(8,128)(2,1)} %get-tuple-element.33), channel_id=1, source_target_pairs={{0,24},{24,0},{48,72},{72,48},{96,120},{120,96},{144,168},{168,144... | collective-permute-start | bytes 1474568 | tf_op jit(solution)/shard_map/ppermute | solution.py:262
  63.9 13.1 %collective-permute-start.9 = (bf16[48,1280]{1,0:T(8,128)(2,1)S(1)}, bf16[48,1280]{1,0:T(8,128)(2,1)S(1)}, u32[]{:S(2)}, u32[]{:S(2)}) collective-permute-start(bf16[48,1280]{1,0:T(8,128)(2,1)S(1)} %get-tuple-element.39), channel_id=1, source_target_pairs={{0,16},{1,17},{2,18},{3,19},{4,20},{5,21},{6,22},{7,23},{8,0},{9,1... | collective-permute-start | bytes 368648 | tf_op jit(solution)/shard_map/ppermute | solution.py:271
  70.2 32.5 %all-to-all-start.1 = ((bf16[8,48,1152]{2,1,0:T(8,128)(2,1)}), bf16[8,48,1152]{2,1,0:T(8,128)(2,1)}, u32[]{:S(2)}, u32[]{:S(2)}) async-start(bf16[8,48,1152]{2,1,0:T(8,128)(2,1)} %bitcast.6), calls=%async_computation.1 | async-start | bytes 1769472 | tf_op jit(solution)/shard_map/all_to_all | solution.py:239
  78.4 11.8 %collective-permute-start.10 = (bf16[96,1280]{1,0:T(8,128)(2,1)S(1)}, bf16[96,1280]{1,0:T(8,128)(2,1)S(1)}, u32[]{:S(2)}, u32[]{:S(2)}) collective-permute-start(bf16[96,1280]{1,0:T(8,128)(2,1)S(1)} %get-tuple-element.41), channel_id=1, source_target_pairs={{0,48},{24,72},{48,0},{72,24},{96,144},{120,168},{144,96},{168,120... | collective-permute-start | bytes 737288 | tf_op jit(solution)/shard_map/ppermute | solution.py:279
  81.8 8.3 %collective-permute-start.11 = (bf16[48,1152]{1,0:T(8,128)(2,1)S(1)}, bf16[48,1152]{1,0:T(8,128)(2,1)S(1)}, u32[]{:S(2)}, u32[]{:S(2)}) collective-permute-start(bf16[48,1152]{1,0:T(8,128)(2,1)S(1)} %get-tuple-element.43), channel_id=1, source_target_pairs={{0,384},{24,216},{48,432},{72,264},{96,480},{120,312},{144,528},{1... | collective-permute-start | bytes 331784 | tf_op jit(solution)/shard_map/ppermute | solution.py:280
  83.8 20.2 %collective-permute-start.13 = (bf16[48,1280]{1,0:T(8,128)(2,1)S(1)}, bf16[48,1280]{1,0:T(8,128)(2,1)S(1)}, u32[]{:S(2)}, u32[]{:S(2)}) collective-permute-start(bf16[48,1280]{1,0:T(8,128)(2,1)S(1)} %get-tuple-element.47), channel_id=1, source_target_pairs={{0,8},{1,9},{2,10},{3,11},{4,12},{5,13},{6,14},{7,15},{8,16},{9,17... | collective-permute-start | bytes 368648 | tf_op jit(solution)/shard_map/ppermute | solution.py:272
  91.0 13.0 %collective-permute-start.12 = (bf16[48,1280]{1,0:T(8,128)(2,1)S(1)}, bf16[48,1280]{1,0:T(8,128)(2,1)S(1)}, u32[]{:S(2)}, u32[]{:S(2)}) collective-permute-start(bf16[48,1280]{1,0:T(8,128)(2,1)S(1)} %get-tuple-element.45), channel_id=1, source_target_pairs={{0,144},{24,168},{48,96},{72,120},{96,48},{120,72},{144,0},{168,24... | collective-permute-start | bytes 368648 | tf_op jit(solution)/shard_map/ppermute | solution.py:285
  103.9 1.0 copy-start
